TPU v7x, 32 devices: a whole 2x2x4 slice. The times are simulated.
32 devices in a mesh: segment: 4 (over z), dp: 8 (over y, x, core).
Axes of the slice: x: 2, y: 2, z: 4, core: 2. Of those that a mesh axis runs over, the one named last changes fastest.
Arguments:
- control_in: bfloat16 [2048, 1536], P('dp'), may hold values from -10 to 10
- base_in: bfloat16 [2048, 2560], P('dp'), may hold values from -6 to 6
- base_update: bfloat16 [4, 2048, 2560], P('segment', 'dp'), may hold values from -4 to 4
- out_gain: float32 [2560], replicated, may hold values from 0.25 to 1.75
- cotangent: bfloat16 [2048, 2560], P('dp'), may hold values from -6 to 6
- w_qkv: bfloat16 [4, 1536, 2304], P('segment', 'dp'), may hold values from -1 to 1
- w_out: bfloat16 [4, 768, 1536], P('segment', 'dp'), may hold values from -0.21875 to 0.21875
- w_hint: bfloat16 [4, 1536, 2560], P('segment', 'dp'), may hold values from -0.15625 to 0.15625
- window_offset: int32 [4, 4], P('segment'), may hold values from -1 to 1
- tile_mask: int32 [4, 4, 4], P('segment'), may hold values 0 or 1
- token_layout: int32 [8, 256], P('dp'), may hold values from 0 to 255, each once within a row
Outputs:
- features: float32 [2048, 2560], P('dp')
- grad_qkv: float32 [4, 1536, 2304], P('segment', 'dp')
- grad_out: float32 [4, 768, 1536], P('segment', 'dp')
- grad_hint: float32 [4, 1536, 2560], P('segment', 'dp')
All inputs are finite; a program needn't handle non-finite values. No bound on the sum of `tile_mask` on one device may be relied on, other than what follows from the above.
Results may differ from a plain program's by a relative error of at most 0.03.
Values may be sent and summed in bfloat16 or wider, within the bound.
No kernel may reach another device: no remote copies, remote signals or barrier semaphores. Data moves between devices by JAX's collectives and lax.ppermute only.
A program may use at most 192 MiB of HBM per device.

v0:
```python
import jax
import jax.numpy as jnp
from jax import lax
from jax.sharding import PartitionSpec as P

HEADS = 6
HEAD = 128
TILE = 64


def passed_along(value, axis, by):
    size = lax.axis_size(axis)
    pairs = [(i, i + by) for i in range(size) if 0 <= i + by < size]
    return lax.ppermute(value, axis, pairs)


def token_mask(offset, mask):
    count = mask.shape[0]
    row_tile = jnp.arange(count)[:, None]
    col_tile = jnp.arange(count)[None, :]
    near_window = jnp.abs(col_tile - row_tile - offset[:, None]) <= 1
    permitted = (row_tile == col_tile) | near_window & (mask == 1)
    return jnp.repeat(jnp.repeat(permitted, TILE, 0), TILE, 1)


def flat_positions(layout):
    count, length = layout.shape
    return (layout + (jnp.arange(count) * length)[:, None]).reshape(-1)


def forward_block(control, positions, permitted, weight_qkv, weight_out, weight_hint):
    total_rows = control.shape[0]
    length = permitted.shape[0]
    count = total_rows // length
    widened = control.astype(jnp.float32)
    inverse = lax.rsqrt(jnp.mean(widened * widened, -1, keepdims=True) + 1e-06)
    normed = (widened * inverse).astype(jnp.bfloat16)
    projected = jnp.dot(normed, weight_qkv, preferred_element_type=jnp.float32).astype(jnp.bfloat16)
    tiled_proj = projected[positions].reshape(count, length, 3, HEADS, HEAD)
    query_rows = tiled_proj[:, :, 0]
    key_rows = tiled_proj[:, :, 1]
    value_rows = tiled_proj[:, :, 2]
    scores = jnp.einsum(
        "cqhe,ckhe->chqk", query_rows, key_rows, preferred_element_type=jnp.float32
    ) * HEAD ** (-0.5)
    scores = jnp.where(permitted, scores, -1e30)
    row_max = jnp.max(scores, -1, keepdims=True)
    shifted = jnp.exp(scores - row_max)
    softmax_out = shifted / jnp.sum(shifted, -1, keepdims=True)
    soft_half = softmax_out.astype(jnp.bfloat16)
    attended = jnp.einsum(
        "chqk,ckhe->cqhe", soft_half, value_rows, preferred_element_type=jnp.float32
    ).astype(jnp.bfloat16)
    attended = attended.reshape(total_rows, HEADS * HEAD)
    merged = jnp.zeros_like(attended).at[positions].set(attended)
    control_out = (
        widened + jnp.dot(merged, weight_out, preferred_element_type=jnp.float32)
    ).astype(jnp.bfloat16)
    hint_term = jnp.dot(control_out, weight_hint, preferred_element_type=jnp.float32)
    return (control_out, hint_term, (control, normed, tiled_proj, softmax_out, merged))


def backward_block(
    saved, control_out, grad_next, grad_summed, positions, weight_qkv, weight_out, weight_hint
):
    control, normed, tiled_proj, softmax_out, merged = saved
    total_rows = control.shape[0]
    count, length = (tiled_proj.shape[0], tiled_proj.shape[1])
    grad_after = (
        grad_next.astype(jnp.float32)
        + jnp.dot(grad_summed, weight_hint.T, preferred_element_type=jnp.float32)
    ).astype(jnp.bfloat16)
    grad_hint = jnp.dot(control_out.T, grad_summed, preferred_element_type=jnp.float32)
    grad_out = jnp.dot(merged.T, grad_after, preferred_element_type=jnp.float32)
    grad_merged = jnp.dot(grad_after, weight_out.T, preferred_element_type=jnp.float32).astype(
        jnp.bfloat16
    )
    grad_tiled = grad_merged[positions].reshape(count, length, HEADS, HEAD)
    query_rows = tiled_proj[:, :, 0]
    key_rows = tiled_proj[:, :, 1]
    value_rows = tiled_proj[:, :, 2]
    soft_half = softmax_out.astype(jnp.bfloat16)
    grad_values = jnp.einsum(
        "chqk,cqhe->ckhe", soft_half, grad_tiled, preferred_element_type=jnp.float32
    ).astype(jnp.bfloat16)
    grad_probs = jnp.einsum(
        "cqhe,ckhe->chqk", grad_tiled, value_rows, preferred_element_type=jnp.float32
    )
    grad_scores = (
        softmax_out
        * (grad_probs - jnp.sum(grad_probs * softmax_out, -1, keepdims=True))
        * HEAD ** (-0.5)
    )
    grad_scores = grad_scores.astype(jnp.bfloat16)
    grad_queries = jnp.einsum(
        "chqk,ckhe->cqhe", grad_scores, key_rows, preferred_element_type=jnp.float32
    ).astype(jnp.bfloat16)
    grad_keys = jnp.einsum(
        "chqk,cqhe->ckhe", grad_scores, query_rows, preferred_element_type=jnp.float32
    ).astype(jnp.bfloat16)
    grad_stack = jnp.stack((grad_queries, grad_keys, grad_values), 2).reshape(
        total_rows, 3 * HEADS * HEAD
    )
    grad_proj = jnp.zeros_like(grad_stack).at[positions].set(grad_stack)
    grad_qkv = jnp.dot(normed.T, grad_proj, preferred_element_type=jnp.float32)
    grad_normed = jnp.dot(grad_proj, weight_qkv.T, preferred_element_type=jnp.float32)
    widened = control.astype(jnp.float32)
    inverse = lax.rsqrt(jnp.mean(widened * widened, -1, keepdims=True) + 1e-06)
    through = inverse * grad_normed - widened * inverse**3 * jnp.mean(
        grad_normed * widened, -1, keepdims=True
    )
    grad_control = (grad_after.astype(jnp.float32) + through).astype(jnp.bfloat16)
    return (grad_control, (grad_qkv, grad_out, grad_hint))


def norm_grad(summed, gain, cotangent):
    inverse = lax.rsqrt(jnp.mean(summed * summed, -1, keepdims=True) + 1e-06)
    features = summed * inverse * gain
    grad_normed = cotangent.astype(jnp.float32) * gain
    grad_summed = inverse * grad_normed - summed * inverse**3 * jnp.mean(
        grad_normed * summed, -1, keepdims=True
    )
    return (features, grad_summed.astype(jnp.bfloat16))


def shards(
    control_in,
    base_in,
    base_update,
    out_gain,
    cotangent,
    w_qkv,
    w_out,
    w_hint,
    window_offset,
    tile_mask,
    token_layout,
):
    segments = lax.axis_size("segment")
    mine = lax.axis_index("segment")
    weight_qkv, weight_out, weight_hint = (
        lax.all_gather(w_qkv[0], "dp", axis=0, tiled=True),
        lax.all_gather(w_out[0], "dp", axis=0, tiled=True),
        lax.all_gather(w_hint[0], "dp", axis=0, tiled=True),
    )
    permitted = token_mask(window_offset[0], tile_mask[0])
    total_rows, width = control_in.shape
    count, length = token_layout.shape
    feat_width = base_in.shape[1]
    factor = float(total_rows * lax.axis_size("dp")) ** (-0.5)
    positions = flat_positions(token_layout)
    empty_state = (
        jnp.zeros((total_rows, width), jnp.bfloat16),
        jnp.zeros((total_rows, width), jnp.bfloat16),
        jnp.zeros((count, length, 3, HEADS, HEAD), jnp.bfloat16),
        jnp.zeros((count, HEADS, length, length), jnp.float32),
        jnp.zeros((total_rows, HEADS * HEAD), jnp.bfloat16),
    )
    empty_out = jnp.zeros((total_rows, width), jnp.bfloat16)
    empty_hint = jnp.zeros((total_rows, feat_width), jnp.float32)

    def run_forward(carry):
        control_out, hint_term, saved = forward_block(
            carry[0], positions, permitted, weight_qkv, weight_out, weight_hint
        )
        return (control_out, saved, control_out, hint_term)

    def keep_forward(carry):
        return carry

    def forward_turn(tick, carry):
        result = lax.cond(mine == tick, run_forward, keep_forward, carry)
        passed = passed_along(result[0], "segment", 1)
        return (passed,) + result[1:]

    carry = lax.fori_loop(
        0, segments, forward_turn, (control_in, empty_state, empty_out, empty_hint)
    )
    saved, control_out, hint_term = (carry[1], carry[2], carry[3])
    term = base_update[0].astype(jnp.float32) + hint_term
    summed = base_in.astype(jnp.float32) + lax.psum(term.astype(jnp.bfloat16), "segment").astype(
        jnp.float32
    )
    features, grad_summed = norm_grad(summed, out_gain, cotangent)
    empty_grads = (
        jnp.zeros(weight_qkv.shape, jnp.float32),
        jnp.zeros(weight_out.shape, jnp.float32),
        jnp.zeros(weight_hint.shape, jnp.float32),
    )

    def run_backward(carry_back):
        return backward_block(
            saved,
            control_out,
            carry_back[0],
            grad_summed,
            positions,
            weight_qkv,
            weight_out,
            weight_hint,
        )

    def keep_backward(carry_back):
        return carry_back

    def backward_turn(tick, carry_back):
        result = lax.cond(mine == segments - 1 - tick, run_backward, keep_backward, carry_back)
        passed = passed_along(result[0], "segment", -1)
        return (passed, result[1])

    start_back = (jnp.zeros((total_rows, width), jnp.bfloat16), empty_grads)
    local_grads = lax.fori_loop(0, segments, backward_turn, start_back)[1]
    summed_grads = (
        lax.psum_scatter(
            local_grads[0].astype(jnp.bfloat16), "dp", scatter_dimension=0, tiled=True
        ).astype(jnp.float32),
        lax.psum_scatter(
            local_grads[1].astype(jnp.bfloat16), "dp", scatter_dimension=0, tiled=True
        ).astype(jnp.float32),
        lax.psum_scatter(
            local_grads[2].astype(jnp.bfloat16), "dp", scatter_dimension=0, tiled=True
        ).astype(jnp.float32),
    )
    return (
        features,
        (summed_grads[0] * factor)[None],
        (summed_grads[1] * factor)[None],
        (summed_grads[2] * factor)[None],
    )


def solution(mesh):
    placed = (
        P("dp", None),
        P("dp", None),
        P("segment", "dp", None),
        P(),
        P("dp", None),
        P("segment", "dp", None),
        P("segment", "dp", None),
        P("segment", "dp", None),
        P("segment", None),
        P("segment", None, None),
        P("dp", None),
    )
    return jax.shard_map(
        shards,
        mesh=mesh,
        in_specs=placed,
        out_specs=(
            P("dp", None),
            P("segment", "dp", None),
            P("segment", "dp", None),
            P("segment", "dp", None),
        ),
        check_vma=False,
    )
```

profile of v0, /device:TPU:0, one launch (start us, length us, event | category | flops | bytes accessed | tf_op | source)
XLA Modules:
  0.0 897.0 jit_solution(5025350985412095998)
XLA Ops:
  10.4 31.2 %all-gather.9.cloned.1.call-done = bf16[1,768,1536]{2,1,0:T(8,128)(2,1)} async-done(((bf16[1,96,1536]{2,1,0:T(8,128)(2,1)}), bf16[1,768,1536]{2,1,0:T(8,128)(2,1)}) %all-gather.9.cloned.1.call-update) | async-done | bytes 2359312 | tf_op jit(solution)/shard_map/all_gather | solution.py:143
  41.7 50.8 %all-gather.7.cloned.1.call-done = bf16[1,1536,2304]{2,1,0:T(8,128)(2,1)} async-done(((bf16[1,192,2304]{2,1,0:T(8,128)(2,1)}), bf16[1,1536,2304]{2,1,0:T(8,128)(2,1)}) %all-gather.7.cloned.1.call-update) | async-done | bytes 7077904 | tf_op jit(solution)/shard_map/all_gather | solution.py:142
  92.4 54.1 %all-gather.11.cloned.1.call-done = bf16[1,1536,2560]{2,1,0:T(8,128)(2,1)} async-done(((bf16[1,192,2560]{2,1,0:T(8,128)(2,1)}), bf16[1,1536,2560]{2,1,0:T(8,128)(2,1)}) %all-gather.11.cloned.1.call-update) | async-done | bytes 7864336 | tf_op jit(solution)/shard_map/all_gather | solution.py:144
  150.5 1.8 broadcast_in_dim.63
  152.3 177.0 %while.48 = (s32[]{:T(128)}, bf16[256,1536]{1,0:T(8,128)(2,1)S(1)}, bf16[256,1536]{1,0:T(8,128)(2,1)}, bf16[256,1536]{1,0:T(8,128)(2,1)}, bf16[1,256,3,6,128]{1,...) while((s32[]{:T(128)}, bf16[256,1536]{1,0:T(8,128)(2,1)S(1)}, ...), condition=%wide.region_7.8_spmd.clone, body=%wide.region_0.7_spmd.clone.sunk | while | flops 4739436544 | bytes 56196560 | solution.py:176
  153.6 30.7 %conditional.6 = (bf16[256,1536]{1,0:T(8,128)(2,1)}, bf16[256,1536]{1,0:T(8,128)(2,1)}, bf16[256,1536]{1,0:T(8,128)(2,1)}, bf16[1,256,3,6,128]{1,4,3,2,0:T(8,128...) conditional(s32[]{:T(128)} %convert_element_type.230, ...), branch_computations={%region_1.0_spmd, %region_2.6_spmd} | conditional | flops 4739436544 | bytes 52983960 | solution.py:172
  154.9 5.3 convolution_convert_fusion
  163.2 1.8 fusion.44
  166.7 2.2 convolution_convert_fusion.1
  169.1 2.4 scatter_custom_fusion
  171.4 3.5 fusion.3
  174.9 7.2 fusion.45
  182.1 2.2 copy.74
  185.6 17.8 %collective-permute-done.1 = bf16[256,1536]{1,0:T(8,128)(2,1)S(1)} collective-permute-done((bf16[256,1536]{1,0:T(8,128)(2,1)}, bf16[256,1536]{1,0:T(8,128)(2,1)S(1)}, u32[]{:S(2)}, u32[]{:S(2)}) %collective-permute-start.1) | collective-permute-done | bytes 786464 | tf_op jit(solution)/shard_map/while/body/eval_jaxpr/ppermute | solution.py:14
  205.5 34.1 %collective-permute-start.1 = (bf16[256,1536]{1,0:T(8,128)(2,1)}, bf16[256,1536]{1,0:T(8,128)(2,1)S(1)}, u32[]{:S(2)}, u32[]{:S(2)}) collective-permute-start(bf16[256,1536]{1,0:T(8,128)(2,1)} %get-tuple-element.999), channel_id=1, source_target_pairs={{0,8},{8,16},{16,24},{1,9},{9,17},{17,25},{2,10},{10,18},{18,26},{... | collective-permute-start | bytes 2359304 | tf_op jit(solution)/shard_map/while/body/eval_jaxpr/ppermute | solution.py:14
  239.7 17.0 %collective-permute-done.1 = bf16[256,1536]{1,0:T(8,128)(2,1)S(1)} collective-permute-done((bf16[256,1536]{1,0:T(8,128)(2,1)}, bf16[256,1536]{1,0:T(8,128)(2,1)S(1)}, u32[]{:S(2)}, u32[]{:S(2)}) %collective-permute-start.1) | collective-permute-done | bytes 786464 | tf_op jit(solution)/shard_map/while/body/eval_jaxpr/ppermute | solution.py:14
  258.8 4.3 collective-permute-start.1
  263.2 16.1 %collective-permute-done.1 = bf16[256,1536]{1,0:T(8,128)(2,1)S(1)} collective-permute-done((bf16[256,1536]{1,0:T(8,128)(2,1)}, bf16[256,1536]{1,0:T(8,128)(2,1)S(1)}, u32[]{:S(2)}, u32[]{:S(2)}) %collective-permute-start.1) | collective-permute-done | bytes 786464 | tf_op jit(solution)/shard_map/while/body/eval_jaxpr/ppermute | solution.py:14
  281.5 32.3 %collective-permute-start.1 = (bf16[256,1536]{1,0:T(8,128)(2,1)}, bf16[256,1536]{1,0:T(8,128)(2,1)S(1)}, u32[]{:S(2)}, u32[]{:S(2)}) collective-permute-start(bf16[256,1536]{1,0:T(8,128)(2,1)} %get-tuple-element.999), channel_id=1, source_target_pairs={{0,8},{8,16},{16,24},{1,9},{9,17},{17,25},{2,10},{10,18},{18,26},{... | collective-permute-start | bytes 2359304 | tf_op jit(solution)/shard_map/while/body/eval_jaxpr/ppermute | solution.py:14
  313.8 15.5 %collective-permute-done.1 = bf16[256,1536]{1,0:T(8,128)(2,1)S(1)} collective-permute-done((bf16[256,1536]{1,0:T(8,128)(2,1)}, bf16[256,1536]{1,0:T(8,128)(2,1)S(1)}, u32[]{:S(2)}, u32[]{:S(2)}) %collective-permute-start.1) | collective-permute-done | bytes 786464 | tf_op jit(solution)/shard_map/while/body/eval_jaxpr/ppermute | solution.py:14
  329.3 3.5 fusion.41
  334.4 89.1 %all-reduce.2.cloned.1.call-done = bf16[256,2560]{1,0:T(8,128)(2,1)} async-done(((bf16[256,2560]{1,0:T(8,128)(2,1)}), bf16[256,2560]{1,0:T(8,128)(2,1)}) %all-reduce.2.cloned.1.call-update) | async-done | bytes 1310736 | tf_op jit(solution)/shard_map/psum | solution.py:181
  423.6 3.1 multiply_reduce_fusion
  426.8 3.2 subtract_convert_fusion
  432.5 3.3 broadcast_in_dim.66
  435.9 3.7 broadcast_in_dim.68
  439.6 259.4 %while.47 = (s32[]{:T(128)}, bf16[256,1536]{1,0:T(8,128)(2,1)}, bf16[1536,2304]{0,1:T(8,128)(2,1)}, bf16[768,1536]{0,1:T(8,128)(2,1)}, bf16[1536,2560]{1,0:T(8,1...) while((s32[]{:T(128)}, bf16[256,1536]{1,0:T(8,128)(2,1)}, ...), condition=%wide.region_18.19_spmd, body=%wide.region_11.18_spmd.sunk | while | flops 9272034304 | bytes 100301824 | solution.py:212
  440.8 19.9 %collective-permute-done = bf16[256,1536]{1,0:T(8,128)(2,1)S(1)} collective-permute-done((bf16[256,1536]{1,0:T(8,128)(2,1)}, bf16[256,1536]{1,0:T(8,128)(2,1)S(1)}, u32[]{:S(2)}, u32[]{:S(2)}) %collective-permute-start) | collective-permute-done | bytes 786464 | tf_op jit(solution)/shard_map/while/body/eval_jaxpr/ppermute | solution.py:14
  462.9 19.0 %collective-permute-done = bf16[256,1536]{1,0:T(8,128)(2,1)S(1)} collective-permute-done((bf16[256,1536]{1,0:T(8,128)(2,1)}, bf16[256,1536]{1,0:T(8,128)(2,1)S(1)}, u32[]{:S(2)}, u32[]{:S(2)}) %collective-permute-start) | collective-permute-done | bytes 786464 | tf_op jit(solution)/shard_map/while/body/eval_jaxpr/ppermute | solution.py:14
  484.2 149.4 %collective-permute-done = bf16[256,1536]{1,0:T(8,128)(2,1)S(1)} collective-permute-done((bf16[256,1536]{1,0:T(8,128)(2,1)}, bf16[256,1536]{1,0:T(8,128)(2,1)S(1)}, u32[]{:S(2)}, u32[]{:S(2)}) %collective-permute-start) | collective-permute-done | bytes 786464 | tf_op jit(solution)/shard_map/while/body/eval_jaxpr/ppermute | solution.py:14
  634.4 44.3 %conditional.5 = ((bf16[256,1536]{1,0:T(8,128)(2,1)}, bf16[1536,2304]{0,1:T(8,128)(2,1)}, bf16[768,1536]{0,1:T(8,128)(2,1)}, bf16[1536,2560]{1,0:T(8,128)(2,1)})) conditional(s32[]{:T(128)} %convert_element_type.229, (bf16[256,1536]{1,0:T(8,128)(2,1)}, bf16[1536,2304]{0,1:T(8,128)(2,1)}, bf16[768,1536]{0,1:T(8,128)(2,1)}, ...), branch_computations={%region_12.12_spmd, %region_13.17_spmd} | conditional | flops 9272034304 | bytes 95582864 | solution.py:207
  634.4 6.1 fusion.20
  643.9 2.4 copy.35
  651.6 3.3 scatter_custom_fusion.1
  655.0 5.3 fusion.21
  660.2 2.5 fusion.25
  662.8 3.2 convolution_bitcast_fusion.1
  666.0 6.2 convolution_bitcast_fusion
  672.1 6.5 fusion.46
  680.0 18.1 %collective-permute-done = bf16[256,1536]{1,0:T(8,128)(2,1)S(1)} collective-permute-done((bf16[256,1536]{1,0:T(8,128)(2,1)}, bf16[256,1536]{1,0:T(8,128)(2,1)S(1)}, u32[]{:S(2)}, u32[]{:S(2)}) %collective-permute-start) | collective-permute-done | bytes 786464 | tf_op jit(solution)/shard_map/while/body/eval_jaxpr/ppermute | solution.py:14
  699.0 4.3 copy.44
  703.4 10.4 %copy.43 = bf16[1536,2304]{1,0:T(8,128)(2,1)} copy(bf16[1536,2304]{0,1:T(8,128)(2,1)} %get-tuple-element.647) | data formatting | bytes 14155776 | tf_op jit(solution)/shard_map/while | solution.py:212
  714.6 30.7 %reduce-scatter.6.cloned.1.call-done = bf16[96,1536]{1,0:T(8,128)(2,1)} async-done(((bf16[768,1536]{1,0:T(8,128)(2,1)}), bf16[96,1536]{1,0:T(8,128)(2,1)}) %reduce-scatter.6.cloned.1.call-update) | async-done | bytes 294928 | tf_op jit(solution)/shard_map/reduce_scatter | solution.py:217
  745.3 1.8 multiply_bitcast_fusion.2
  747.1 67.5 %reduce-scatter.4.cloned.1.call-done = bf16[192,2304]{1,0:T(8,128)(2,1)} async-done(((bf16[1536,2304]{1,0:T(8,128)(2,1)}), bf16[192,2304]{1,0:T(8,128)(2,1)}) %reduce-scatter.4.cloned.1.call-update) | async-done | bytes 884752 | tf_op jit(solution)/shard_map/reduce_scatter | solution.py:214
  814.6 2.5 multiply_bitcast_fusion.1
  817.1 70.3 %reduce-scatter.8.cloned.1.call-done = bf16[192,2560]{1,0:T(8,128)(2,1)} async-done(((bf16[1536,2560]{1,0:T(8,128)(2,1)}), bf16[192,2560]{1,0:T(8,128)(2,1)}) %reduce-scatter.8.cloned.1.call-update) | async-done | bytes 983056 | tf_op jit(solution)/shard_map/reduce_scatter | solution.py:220
  887.5 2.7 multiply_bitcast_fusion
  (103 shorter events, 47.4 us)
Async XLA Ops:
  7.2 2.3 copy-start.13
  7.2 2.3 copy-start.12
  7.2 34.5 %all-gather.9.cloned.1.call-start = ((), (), s32[]{:S(2)}) async-start(), calls=%async_computation.8 | async-start | bytes 2654208 | tf_op jit(solution)/shard_map/all_gather | solution.py:143
  7.9 84.5 %all-gather.7.cloned.1.call-start = ((), (), s32[]{:S(2)}) async-start(), calls=%async_computation.7 | async-start | bytes 7962624 | tf_op jit(solution)/shard_map/all_gather | solution.py:142
  8.7 137.9 %all-gather.11.cloned.1.call-start = ((), (), s32[]{:S(2)}) async-start(), calls=%async_computation.9 | async-start | bytes 8847360 | tf_op jit(solution)/shard_map/all_gather | solution.py:144
  9.4 414.2 %all-reduce.2.cloned.1.call-start = ((), (), s32[]{:S(2)}) async-start(), calls=%async_computation.3 | async-start | bytes 2621440 | tf_op jit(solution)/shard_map/psum | solution.py:181
  150.4 1.8 copy-start
  150.5 1.8 copy-start.10
  161.6 1.6 copy-start.9
  162.3 2.8 copy-start.7
  182.1 2.2 copy-start.8
  184.3 19.1 %collective-permute-start.1 = (bf16[256,1536]{1,0:T(8,128)(2,1)}, bf16[256,1536]{1,0:T(8,128)(2,1)S(1)}, u32[]{:S(2)}, u32[]{:S(2)}) collective-permute-start(bf16[256,1536]{1,0:T(8,128)(2,1)} %get-tuple-element.999), channel_id=1, source_target_pairs={{0,8},{8,16},{16,24},{1,9},{9,17},{17,25},{2,10},{10,18},{18,26},{... | collective-permute-start | bytes 2359304 | tf_op jit(solution)/shard_map/while/body/eval_jaxpr/ppermute | solution.py:14
  205.5 51.1 %collective-permute-start.1 = (bf16[256,1536]{1,0:T(8,128)(2,1)}, bf16[256,1536]{1,0:T(8,128)(2,1)S(1)}, u32[]{:S(2)}, u32[]{:S(2)}) collective-permute-start(bf16[256,1536]{1,0:T(8,128)(2,1)} %get-tuple-element.999), channel_id=1, source_target_pairs={{0,8},{8,16},{16,24},{1,9},{9,17},{17,25},{2,10},{10,18},{18,26},{... | collective-permute-start | bytes 2359304 | tf_op jit(solution)/shard_map/while/body/eval_jaxpr/ppermute | solution.py:14
  258.8 20.4 %collective-permute-start.1 = (bf16[256,1536]{1,0:T(8,128)(2,1)}, bf16[256,1536]{1,0:T(8,128)(2,1)S(1)}, u32[]{:S(2)}, u32[]{:S(2)}) collective-permute-start(bf16[256,1536]{1,0:T(8,128)(2,1)} %get-tuple-element.999), channel_id=1, source_target_pairs={{0,8},{8,16},{16,24},{1,9},{9,17},{17,25},{2,10},{10,18},{18,26},{... | collective-permute-start | bytes 2359304 | tf_op jit(solution)/shard_map/while/body/eval_jaxpr/ppermute | solution.py:14
  281.5 47.8 %collective-permute-start.1 = (bf16[256,1536]{1,0:T(8,128)(2,1)}, bf16[256,1536]{1,0:T(8,128)(2,1)S(1)}, u32[]{:S(2)}, u32[]{:S(2)}) collective-permute-start(bf16[256,1536]{1,0:T(8,128)(2,1)} %get-tuple-element.999), channel_id=1, source_target_pairs={{0,8},{8,16},{16,24},{1,9},{9,17},{17,25},{2,10},{10,18},{18,26},{... | collective-permute-start | bytes 2359304 | tf_op jit(solution)/shard_map/while/body/eval_jaxpr/ppermute | solution.py:14
  332.8 90.8 %copy-start.11 = (f32[2560]{0:T(1024)S(1)}, f32[2560]{0:T(1024)}, u32[]{:S(2)}) copy-start(f32[2560]{0:T(1024)} %param.22) | copy-start | bytes 30724
  332.8 412.5 %reduce-scatter.6.cloned.1.call-start = ((), (), s32[]{:S(2)}) async-start(), calls=%async_computation.5 | async-start | bytes 2654208 | tf_op jit(solution)/shard_map/reduce_scatter | solution.py:217
  423.6 3.1 copy-start.4
  423.6 3.1 copy-start.5
  423.6 3.3 copy-start.6
  439.6 21.2 %collective-permute-start = (bf16[256,1536]{1,0:T(8,128)(2,1)}, bf16[256,1536]{1,0:T(8,128)(2,1)S(1)}, u32[]{:S(2)}, u32[]{:S(2)}) collective-permute-start(bf16[256,1536]{1,0:T(8,128)(2,1)} %get-tuple-element.980), channel_id=1, source_target_pairs={{8,0},{16,8},{24,16},{9,1},{17,9},{25,17},{10,2},{18,10},{26,18},{... | collective-permute-start | bytes 2359304 | tf_op jit(solution)/shard_map/while/body/eval_jaxpr/ppermute | solution.py:14
  461.7 20.3 %collective-permute-start = (bf16[256,1536]{1,0:T(8,128)(2,1)}, bf16[256,1536]{1,0:T(8,128)(2,1)S(1)}, u32[]{:S(2)}, u32[]{:S(2)}) collective-permute-start(bf16[256,1536]{1,0:T(8,128)(2,1)} %get-tuple-element.980), channel_id=1, source_target_pairs={{8,0},{16,8},{24,16},{9,1},{17,9},{25,17},{10,2},{18,10},{26,18},{... | collective-permute-start | bytes 2359304 | tf_op jit(solution)/shard_map/while/body/eval_jaxpr/ppermute | solution.py:14
  482.9 150.7 %collective-permute-start = (bf16[256,1536]{1,0:T(8,128)(2,1)}, bf16[256,1536]{1,0:T(8,128)(2,1)S(1)}, u32[]{:S(2)}, u32[]{:S(2)}) collective-permute-start(bf16[256,1536]{1,0:T(8,128)(2,1)} %get-tuple-element.980), channel_id=1, source_target_pairs={{8,0},{16,8},{24,16},{9,1},{17,9},{25,17},{10,2},{18,10},{26,18},{... | collective-permute-start | bytes 2359304 | tf_op jit(solution)/shard_map/while/body/eval_jaxpr/ppermute | solution.py:14
  634.4 6.1 copy-start.14
  647.7 1.3 copy-start.1
  649.0 1.0 copy-start.3
  666.0 6.2 copy-start.2
  678.7 19.4 %collective-permute-start = (bf16[256,1536]{1,0:T(8,128)(2,1)}, bf16[256,1536]{1,0:T(8,128)(2,1)S(1)}, u32[]{:S(2)}, u32[]{:S(2)}) collective-permute-start(bf16[256,1536]{1,0:T(8,128)(2,1)} %get-tuple-element.980), channel_id=1, source_target_pairs={{8,0},{16,8},{24,16},{9,1},{17,9},{25,17},{10,2},{18,10},{26,18},{... | collective-permute-start | bytes 2359304 | tf_op jit(solution)/shard_map/while/body/eval_jaxpr/ppermute | solution.py:14
  703.3 111.3 %reduce-scatter.4.cloned.1.call-start = ((), (), s32[]{:S(2)}) async-start(), calls=%async_computation.4 | async-start | bytes 7962624 | tf_op jit(solution)/shard_map/reduce_scatter | solution.py:214
  713.8 173.6 %reduce-scatter.8.cloned.1.call-start = ((), (), s32[]{:S(2)}) async-start(), calls=%async_computation.6 | async-start | bytes 8847360 | tf_op jit(solution)/shard_map/reduce_scatter | solution.py:220
Sparse Core Ops, SparseCore 0:
  9.9 31.7 all-gather.8
  43.5 48.8 all-gather.6
  94.3 52.1 all-gather.10
  332.9 90.5 all-reduce.1
  703.4 41.8 reduce-scatter.5
  749.1 65.4 reduce-scatter.3
  818.1 69.3 reduce-scatter.7
where the time goes:
time: 898 us; the launch traced here: 897 us
  waiting for transfers between devices  669 us (74%)
  starting transfers between devices  77.7 us (9%)
  local copies, waits for them, and re-layouts  61.4 us (7%)
  matrix products  51.2 us (6%)
  other arithmetic  22.8 us (3%)
  between operations  14.2 us (2%)
    ppermute x8, waiting for transfers between devices, passed_along(): return lax.ppermute(value, axis, pairs)  273 us
    psum x1, waiting for transfers between devices, shards(): lax.psum(term.astype(jnp.bfloat16), 'segment').astype(jnp.float32)  89.1 us
    ppermute x8, starting transfers between devices, passed_along(): return lax.ppermute(value, axis, pairs)  77.2 us
    reduce_scatter x1, waiting for transfers between devices, shards(): lax.psum_scatter(local_grads[2].astype(jnp.bfloat16), 'dp', scatter_dimen...  70.3 us
    reduce_scatter x1, waiting for transfers between devices, shards(): lax.psum_scatter(local_grads[0].astype(jnp.bfloat16), 'dp', scatter_dimen...  67.5 us
    all_gather x1, waiting for transfers between devices, shards(): lax.all_gather(w_hint[0], 'dp', axis=0, tiled=True)  54.1 us
    all_gather x1, waiting for transfers between devices, shards(): lax.all_gather(w_qkv[0], 'dp', axis=0, tiled=True)  50.8 us
    all_gather x1, waiting for transfers between devices, shards(): lax.all_gather(w_out[0], 'dp', axis=0, tiled=True)  31.2 us
  transfers between devices with their start and end apart: 15, of which 15 were waited for; matrix products, arithmetic and copies ran while one was open for 2% of the time, Pallas kernels for 0%

commit v1 on v0

v1 whole, which is shorter than its diff:
```python
import functools

import jax
import jax.numpy as jnp
from jax import lax
from jax.experimental import pallas as pl
from jax.experimental.pallas import tpu as pltpu
from jax.sharding import PartitionSpec as P

HEADS = 6
HEAD = 128
TILE = 64
HD = HEADS * HEAD
SCALE = HEAD ** (-0.5)
BF = jnp.bfloat16
F32 = jnp.float32
ANY = pl.BlockSpec(memory_space=pl.ANY)
HBM = pl.BlockSpec(memory_space=pltpu.HBM)
SMEM = pl.BlockSpec(memory_space=pltpu.SMEM)
MIB = 1024 * 1024
SECTION_VMEM = 56 * MIB
LAND_VMEM = 46 * MIB
NO_COST = pl.CostEstimate(flops=0, bytes_accessed=0, transcendentals=0)


def mm(a, b):
    return jnp.dot(a, b, preferred_element_type=F32)


def mm_bt(a, b):
    return lax.dot_general(a, b, (((1,), (1,)), ((), ())), preferred_element_type=F32)


def mm_at(a, b):
    return lax.dot_general(a, b, (((0,), (0,)), ((), ())), preferred_element_type=F32)


def token_bias(offset, mask, layout):
    count = mask.shape[0]
    length = layout.shape[0]
    row_tile = jnp.arange(count)[:, None]
    col_tile = jnp.arange(count)[None, :]
    near_window = jnp.abs(col_tile - row_tile - offset[:, None]) <= 1
    permitted = ((row_tile == col_tile) | near_window & (mask == 1)).astype(F32)
    tile_of_position = jnp.arange(length) // TILE
    placed = layout[None, :] == jnp.arange(length)[:, None]
    tile_of_token = jnp.sum(jnp.where(placed, tile_of_position[None, :], 0), 1)
    member = (tile_of_token[:, None] == jnp.arange(count)[None, :]).astype(F32)
    pairs = jnp.dot(jnp.dot(member, permitted), member.T)
    return jnp.where(pairs > 0.5, 0.0, -1e30).astype(F32)


def out_pieces(out_rows):
    main, rest = (2 * out_rows // 3, out_rows // 3)
    return (
        (0, main, 0, 0, 0, 2 * HD),
        (main, rest, 0, 0, 2 * HD, HD),
        (main, rest, HD, rest, 2 * HD, HD),
    )


def pack_kernel(qkv, out, packed, sems):
    qkv_rows, out_rows = (qkv.shape[0], out.shape[0])
    copies = [pltpu.make_async_copy(qkv, packed.at[pl.ds(0, qkv_rows)], sems.at[0])]
    for i, (row, rows, col, prow, pcol, cols) in enumerate(out_pieces(out_rows)):
        copies.append(
            pltpu.make_async_copy(
                out.at[pl.ds(row, rows), pl.ds(col, cols)],
                packed.at[pl.ds(qkv_rows + prow, rows), pl.ds(pcol, cols)],
                sems.at[1 + i],
            )
        )
    for copy in copies:
        copy.start()
    for copy in copies:
        copy.wait()


def pack_shard(qkv, out):
    rows = qkv.shape[0] + out.size // qkv.shape[1]
    return pl.pallas_call(
        pack_kernel,
        out_shape=jax.ShapeDtypeStruct((rows, qkv.shape[1]), BF),
        in_specs=[ANY] * 2,
        out_specs=ANY,
        scratch_shapes=[pltpu.SemaphoreType.DMA((4,))],
        compiler_params=pltpu.CompilerParams(vmem_limit_bytes=MIB),
    )(qkv, out)


def phase_bits(bits, core):
    order = list(range(1, bits + 1))
    return order if core == 0 else order[::-1]


def phase_pairs(bits, phase):
    size = lax.axis_size("dp")
    return [(d, d ^ (1 << phase_bits(bits, d % 2)[phase])) for d in range(size)]


def sibling(value):
    size = lax.axis_size("dp")
    return lax.ppermute(value, "dp", [(d, d ^ 1) for d in range(size)])


def gather_shards(shard, bits, beside):
    held, others = ({0: shard}, {})
    for crossed in range(1, bits + 1):
        near = [p for p in held if p.bit_count() == crossed - 1]
        places = [p for p in range(1 << bits) if p.bit_count() == crossed]
        arrived = []
        for p in places:
            phase = p.bit_length() - 1
            arrived.append(lax.ppermute(held[p ^ (1 << phase)], "dp", phase_pairs(bits, phase)))
        swapped = [sibling(held[p]) for p in near]
        arrived, swapped, beside = lax.optimization_barrier((arrived, swapped, beside))
        held.update(zip(places, arrived))
        others.update(zip(near, swapped))
    others[(1 << bits) - 1] = sibling(held[(1 << bits) - 1])
    flips = [
        [
            sum(1 << bit for i, bit in enumerate(phase_bits(bits, core)) if p >> i & 1)
            for p in range(1 << bits)
        ]
        for core in (0, 1)
    ]
    tables = [flips[core] + [1 ^ f for f in flips[1 - core]] for core in (0, 1)]
    mine = lax.axis_index("dp")
    owners = mine ^ jnp.where(mine % 2 == 0, jnp.array(tables[0]), jnp.array(tables[1]))
    order = range(1 << bits)
    shards = [held[p] for p in order] + [others[p] for p in order]
    return shards, owners.astype(jnp.int32), beside


def land_kernel(first, count, owners, *refs):
    packed, (qkv, out, sems) = (refs[:count], refs[-3:])
    cols = qkv.shape[1]
    total_rows = packed[0].shape[0]
    shards = owners.shape[0]
    qkv_rows, out_rows = (qkv.shape[0] // shards, out.shape[0] // shards)
    for i, ref in enumerate(packed):
        owner = owners[first + i]
        start = pl.multiple_of(owner * qkv_rows, 16)
        pltpu.make_async_copy(
            ref.at[pl.ds(0, qkv_rows)], qkv.at[pl.ds(start, qkv_rows)], sems.at[i]
        ).start()
        for row, rows, col, prow, pcol, width in out_pieces(out_rows):
            start = pl.multiple_of(owner * out_rows + row, 16)
            pltpu.make_async_copy(
                ref.at[pl.ds(qkv_rows + prow, rows), pl.ds(pcol, width)],
                out.at[pl.ds(start, rows), pl.ds(col, width)],
                sems.at[i],
            ).start()
    for i, ref in enumerate(packed):
        pltpu.make_async_copy(ref, ref, sems.at[i]).wait()


def land_shards(owners, packed, first, landed, shapes):
    count = len(packed)
    return pl.pallas_call(
        functools.partial(land_kernel, first, count),
        out_shape=[jax.ShapeDtypeStruct(shape, BF) for shape in shapes],
        in_specs=[SMEM] + [ANY] * (count + len(landed)),
        out_specs=[ANY] * 2,
        input_output_aliases={1 + count + i: i for i in range(len(landed))},
        scratch_shapes=[pltpu.SemaphoreType.DMA((count,))],
        compiler_params=pltpu.CompilerParams(vmem_limit_bytes=SECTION_VMEM if landed else LAND_VMEM),
    )(owners, *packed, *landed)


def nothing_kernel(*refs):
    pass


def unwritten(*shapes):
    return pl.pallas_call(
        nothing_kernel,
        out_shape=[jax.ShapeDtypeStruct(shape, kind) for shape, kind in shapes],
        out_specs=[ANY] * len(shapes),
        compiler_params=pltpu.CompilerParams(vmem_limit_bytes=SECTION_VMEM),
    )()


class SectionWeights:
    def __init__(self, qkv, out, qkv_buf, out_buf, sems):
        self.thirds = [
            pltpu.make_async_copy(qkv.at[:, pl.ds(j * HD, HD)], qkv_buf.at[j], sems.at[j])
            for j in range(3)
        ]
        self.out = pltpu.make_async_copy(out, out_buf, sems.at[3])


def call(kernel, outs, out_specs, scratch, args, specs, aliases):
    return pl.pallas_call(
        kernel,
        out_shape=outs,
        in_specs=specs,
        out_specs=out_specs,
        scratch_shapes=scratch,
        input_output_aliases=aliases,
        compiler_params=pltpu.CompilerParams(vmem_limit_bytes=SECTION_VMEM),
        cost_estimate=NO_COST,
    )(*args)


def forward_kernel(deps, flag, x, bias, w_qkv, w_out, *refs):
    refs = refs[6 + deps :]
    outs, bufs, sems, wsems = (refs[:7], refs[7:-2], refs[-2], refs[-1])
    normed_o, inv_o, proj_o, probs_o, att_o, ctl_o, send_o = outs
    xv, bv, qkv_buf, out_buf, normed_v, inv_v, proj_v, probs_v, att_v, ctl_v = bufs

    @pl.when(flag[0] == 1)
    def _():
        weights = SectionWeights(w_qkv, w_out, qkv_buf, out_buf, wsems)
        get_x = pltpu.make_async_copy(x, xv, sems.at[0])
        get_b = pltpu.make_async_copy(bias, bv, sems.at[1])
        puts = []

        def put(value, out):
            puts.append(pltpu.make_async_copy(value, out, sems.at[2 + len(puts)]))
            puts[-1].start()

        get_x.start()
        for copy in weights.thirds:
            copy.start()
        get_b.start()
        weights.out.start()
        get_x.wait()
        wide = xv[...].astype(F32)
        inverse = lax.rsqrt(jnp.mean(wide * wide, -1, keepdims=True) + 1e-06)
        inv_v[...] = jnp.broadcast_to(inverse, inv_v.shape)
        normed_v[...] = (wide * inverse).astype(BF)
        put(normed_v, normed_o)
        put(inv_v, inv_o)
        for j in range(3):
            weights.thirds[j].wait()
            proj_v[:, j * HD : (j + 1) * HD] = mm(normed_v[...], qkv_buf[j]).astype(BF)
        put(proj_v, proj_o)
        get_b.wait()
        for h in range(HEADS):
            q = proj_v[:, h * HEAD : (h + 1) * HEAD]
            k = proj_v[:, HD + h * HEAD : HD + (h + 1) * HEAD]
            v = proj_v[:, 2 * HD + h * HEAD : 2 * HD + (h + 1) * HEAD]
            scores = mm_bt(q, k) * SCALE + bv[...]
            shifted = jnp.exp(scores - jnp.max(scores, -1, keepdims=True))
            probs = (shifted / jnp.sum(shifted, -1, keepdims=True)).astype(BF)
            probs_v[h] = probs
            att_v[:, h * HEAD : (h + 1) * HEAD] = mm(probs, v).astype(BF)
        put(probs_v, probs_o)
        put(att_v, att_o)
        weights.out.wait()
        ctl_v[...] = (xv[...].astype(F32) + mm(att_v[...], out_buf[...])).astype(BF)
        put(ctl_v, send_o)
        put(ctl_v, ctl_o)
        for copy in puts:
            copy.wait()


def forward_section(flag, x, weights, bias, state, deps):
    rows, width = x.shape
    scratch = [
        pltpu.VMEM((rows, width), BF),
        pltpu.VMEM(bias.shape, F32),
        pltpu.VMEM((3, width, HD), BF),
        pltpu.VMEM((HD, width), BF),
    ]
    scratch += [pltpu.VMEM(s.shape, s.dtype) for s in state]
    scratch += [pltpu.SemaphoreType.DMA((9,)), pltpu.SemaphoreType.DMA((4,))]
    outs = call(
        functools.partial(forward_kernel, len(deps)),
        [jax.ShapeDtypeStruct(s.shape, s.dtype) for s in (*state, x)],
        [HBM] * 6 + [ANY],
        scratch,
        (flag, x, bias, *weights, *state, *deps),
        [SMEM, ANY] + [HBM] * 9 + [ANY] * len(deps),
        {5 + i: i for i in range(6)},
    )
    return outs[:6], outs[6]


def hint_kernel(deps, flag, update, ctl, weight, *refs):
    upper, lower, uv, cv, wv, ov, sems = refs[deps:]
    chunks, _, cols = wv.shape
    half = upper.shape[0]

    @pl.when(flag[0] == 1)
    def _():
        gets = [
            pltpu.make_async_copy(ctl, cv, sems.at[0]),
            pltpu.make_async_copy(update, uv, sems.at[1]),
        ]
        weights = [
            pltpu.make_async_copy(weight.at[:, pl.ds(i * cols, cols)], wv.at[i], sems.at[2 + i])
            for i in range(chunks)
        ]
        gets[0].start()
        weights[0].start()
        gets[1].start()
        for copy in weights[1:]:
            copy.start()
        for copy in gets:
            copy.wait()
        puts = []
        for i in range(chunks):
            weights[i].wait()
            at = slice(i * cols, (i + 1) * cols)
            ov[:, at] = (uv[:, at].astype(F32) + mm(cv[...], wv[i])).astype(BF)
            for j, out in enumerate((upper, lower)):
                puts.append(
                    pltpu.make_async_copy(
                        ov.at[pl.ds(j * half, half), pl.ds(i * cols, cols)],
                        out.at[:, pl.ds(i * cols, cols)],
                        sems.at[2 + chunks + 2 * i + j],
                    )
                )
                puts[-1].start()
        for copy in puts:
            copy.wait()


def hint_term(flag, update, ctl, weight, deps):
    rows, feat = update.shape
    width = ctl.shape[1]
    chunks = 4
    full = pltpu.VMEM((rows, feat), BF)
    return call(
        functools.partial(hint_kernel, len(deps)),
        [jax.ShapeDtypeStruct((rows // 2, feat), BF)] * 2,
        [ANY, ANY],
        [
            full,
            pltpu.VMEM((rows, width), BF),
            pltpu.VMEM((chunks, width, feat // chunks), BF),
            full,
            pltpu.SemaphoreType.DMA((2 + 3 * chunks,)),
        ],
        (flag, update, ctl, weight, *deps),
        [SMEM] + [HBM] * 3 + [ANY] * len(deps),
        {},
    )


def add_kernel(one, two, out):
    out[...] = (one[...].astype(F32) + two[...].astype(F32)).astype(BF)


def add_rows(one, two):
    return pl.pallas_call(
        add_kernel,
        out_shape=jax.ShapeDtypeStruct(one.shape, BF),
        compiler_params=pltpu.CompilerParams(vmem_limit_bytes=8 * MIB),
        cost_estimate=NO_COST,
    )(one, two)


def top_kernel(deps, flag, upper, lower, cot, gain, weight, *refs):
    feat_o, gsum_o, gctl_o, sv, cv, gv, wv, feat_v, gsum_v, gctl_v, sems = refs[3 + deps :]
    chunks, step, _ = wv.shape
    half = upper.shape[0]

    @pl.when(flag[0] == 1)
    def _():
        gets = [
            pltpu.make_async_copy(upper, sv.at[pl.ds(0, half)], sems.at[0]),
            pltpu.make_async_copy(lower, sv.at[pl.ds(half, half)], sems.at[6 + chunks]),
            pltpu.make_async_copy(cot, cv, sems.at[1]),
            pltpu.make_async_copy(gain, gv, sems.at[2]),
        ]
        weights = [
            pltpu.make_async_copy(weight.at[pl.ds(i * step, step)], wv.at[i], sems.at[6 + i])
            for i in range(chunks)
        ]
        for copy in gets + weights:
            copy.start()
        for copy in gets:
            copy.wait()
        total = sv[...].astype(F32)
        inverse = lax.rsqrt(jnp.mean(total * total, -1, keepdims=True) + 1e-06)
        feat_v[...] = total * inverse * gv[...]
        put_feat = pltpu.make_async_copy(feat_v, feat_o, sems.at[3])
        put_feat.start()
        total = sv[...].astype(F32)
        grad_normed = cv[...].astype(F32) * gv[...]
        mean = jnp.mean(grad_normed * total, -1, keepdims=True)
        gsum_v[...] = (inverse * grad_normed - total * (inverse**3 * mean)).astype(BF)
        put_gsum = pltpu.make_async_copy(gsum_v, gsum_o, sems.at[4])
        put_gsum.start()
        for i in range(chunks):
            weights[i].wait()
            gctl_v[:, i * step : (i + 1) * step] = mm_bt(gsum_v[...], wv[i]).astype(BF)
        put_gctl = pltpu.make_async_copy(gctl_v, gctl_o, sems.at[5])
        put_gctl.start()
        put_gctl.wait()
        put_gsum.wait()
        put_feat.wait()


def top_section(flag, summed, cot, gain, weight, state, deps):
    rows, feat = cot.shape
    width = weight.shape[0]
    chunks = 3
    full = pltpu.VMEM((rows, feat), BF)
    return call(
        functools.partial(top_kernel, len(deps)),
        [jax.ShapeDtypeStruct(s.shape, s.dtype) for s in state],
        [HBM] * 3,
        [
            full,
            full,
            pltpu.VMEM((1, feat), F32),
            pltpu.VMEM((chunks, width // chunks, feat), BF),
        ]
        + [pltpu.VMEM(s.shape, s.dtype) for s in state]
        + [pltpu.SemaphoreType.DMA((7 + chunks,))],
        (flag, *summed, cot, gain, weight, *state, *deps),
        [SMEM, ANY, ANY] + [HBM] * 6 + [ANY] * len(deps),
        {6 + i: i for i in range(3)},
    )


def backward_kernel(has_next, deps, flag, w_qkv, w_out, *refs):
    if has_next:
        grad_next, refs = (refs[0], refs[1:])
    gctl, normed, inv, proj, probs = refs[:5]
    refs = refs[8 + deps :]
    outs, bufs, sems, wsems = (refs[:3], refs[3:-2], refs[-2], refs[-1])
    gprev_o, after_o, gproj_o = outs
    gv, gnv, qkv_buf, out_buf, normed_v, inv_v, proj_v, probs_v, gatt_v, after_v, gproj_v, acc = bufs

    @pl.when(flag[0] == 1)
    def _():
        get_g = pltpu.make_async_copy(gctl, gv, sems.at[0])
        get_n = pltpu.make_async_copy(grad_next, gnv, sems.at[1]) if has_next else None
        get_normed = pltpu.make_async_copy(normed, normed_v, sems.at[2])
        get_inv = pltpu.make_async_copy(inv, inv_v, sems.at[3])
        get_proj = pltpu.make_async_copy(proj, proj_v, sems.at[4])
        get_probs = pltpu.make_async_copy(probs, probs_v, sems.at[5])
        weights = SectionWeights(w_qkv, w_out, qkv_buf, out_buf, wsems)
        get_g.start()
        if has_next:
            get_n.start()
        weights.out.start()
        get_proj.start()
        get_probs.start()
        get_g.wait()
        if has_next:
            get_n.wait()
            after_v[...] = (gnv[...].astype(F32) + gv[...].astype(F32)).astype(BF)
        else:
            after_v[...] = gv[...]
        put_after = pltpu.make_async_copy(after_v, after_o, sems.at[6])
        put_after.start()
        for copy in weights.thirds:
            copy.start()
        get_normed.start()
        get_inv.start()
        weights.out.wait()
        gatt_v[...] = mm_bt(after_v[...], out_buf[...]).astype(BF)
        get_proj.wait()
        get_probs.wait()
        for h in range(HEADS):
            at = [slice(j * HD + h * HEAD, j * HD + (h + 1) * HEAD) for j in range(3)]
            q, k, v = (proj_v[:, a] for a in at)
            grad = gatt_v[:, at[0]]
            half = probs_v[h]
            wide = half.astype(F32)
            gproj_v[:, at[2]] = mm_at(half, grad).astype(BF)
            grad_probs = mm_bt(grad, v)
            spread = grad_probs - jnp.sum(grad_probs * wide, -1, keepdims=True)
            grad_scores = (wide * spread * SCALE).astype(BF)
            gproj_v[:, at[0]] = mm(grad_scores, k).astype(BF)
            gproj_v[:, at[1]] = mm_at(grad_scores, q).astype(BF)
        put_gproj = pltpu.make_async_copy(gproj_v, gproj_o, sems.at[7])
        put_gproj.start()
        for j in range(3):
            weights.thirds[j].wait()
            part = mm_bt(gproj_v[:, j * HD : (j + 1) * HD], qkv_buf[j])
            if j == 0:
                acc[...] = part
            else:
                acc[...] += part
        get_normed.wait()
        get_inv.wait()
        wide = normed_v[...].astype(F32)
        mean = jnp.mean(acc[...] * wide, -1, keepdims=True)
        through = inv_v[:, :1] * (acc[...] - normed_v[...].astype(F32) * mean)
        gv[...] = (after_v[...].astype(F32) + through).astype(BF)
        put_gprev = pltpu.make_async_copy(gv, gprev_o, sems.at[8])
        put_gprev.start()
        put_gprev.wait()
        put_after.wait()
        put_gproj.wait()


def backward_section(flag, grad_next, gctl, weights, saved, state, deps):
    rows, width = gctl.shape
    tail = [] if grad_next is None else [grad_next]
    normed, inv, proj, probs = saved
    args = (flag, *weights, *tail, gctl, normed, inv, proj, probs, *state, *deps)
    first = 8 + len(tail)
    full = pltpu.VMEM((rows, width), BF)
    return call(
        functools.partial(backward_kernel, bool(tail), len(deps)),
        [jax.ShapeDtypeStruct(s.shape, s.dtype) for s in state],
        [ANY, HBM, HBM],
        [
            full,
            full,
            pltpu.VMEM((3, width, HD), BF),
            pltpu.VMEM((HD, width), BF),
            full,
            pltpu.VMEM(inv.shape, F32),
            pltpu.VMEM(proj.shape, BF),
            pltpu.VMEM(probs.shape, BF),
            pltpu.VMEM((rows, HD), BF),
            full,
            pltpu.VMEM(proj.shape, BF),
            pltpu.VMEM((rows, width), F32),
            pltpu.SemaphoreType.DMA((9,)),
            pltpu.SemaphoreType.DMA((4,)),
        ],
        args,
        [SMEM, HBM, HBM] + [ANY] * len(tail) + [HBM] * 5 + [ANY] + [HBM] * 2 + [ANY] * len(deps),
        {first + i: i for i in range(1, len(state))},
    )


def out_value_kernel(att, after, after_sib, norm, gproj, gproj_sib, low, high):
    owners, rows, cols = (low.shape[0] * 2, low.shape[1] // 2, low.shape[2])
    clip = after.shape[0]
    values = slice(2 * HD, 3 * HD)
    out = mm(att[:, :clip], after[...]) + mm(att[:, clip:], after_sib[...])
    value = mm(norm[:, :clip], gproj[:, values]) + mm(norm[:, clip:], gproj_sib[:, values])
    for p in range(owners):
        to, at = ((low, p) if p < owners // 2 else (high, p - owners // 2))
        to[at, :rows] = out[p * rows : (p + 1) * rows].astype(BF)
        first = 2 * p * rows
        to[at, rows:, :HD] = value[first : first + rows].astype(BF)
        to[at, rows:, HD:] = value[first + rows : first + 2 * rows].astype(BF)


def product_kernel(norm, gproj, gproj_sib, low, high):
    owners, rows, cols = (low.shape[0] * 2, low.shape[1], low.shape[2])
    clip = gproj.shape[0]
    for p in range(owners):
        to, at = ((low, p) if p < owners // 2 else (high, p - owners // 2))
        mine = norm[p * rows : (p + 1) * rows, :clip]
        other = norm[p * rows : (p + 1) * rows, clip:]
        total = mm(mine, gproj[:, :cols]) + mm(other, gproj_sib[:, :cols])
        to[at] = total.astype(BF)


def owner_products(kernel, args, owners, rows, cols):
    block = jax.ShapeDtypeStruct((owners // 2, rows, cols), BF)
    return pl.pallas_call(
        kernel,
        out_shape=[block, block],
        compiler_params=pltpu.CompilerParams(vmem_limit_bytes=32 * MIB),
        cost_estimate=NO_COST,
    )(*args)


def after_kernel(upper, lower, done, upper_out, lower_out):
    pass


def held_until(values, done):
    return pl.pallas_call(
        after_kernel,
        out_shape=[jax.ShapeDtypeStruct(v.shape, v.dtype) for v in values],
        in_specs=[ANY] * 3,
        out_specs=[ANY] * 2,
        input_output_aliases={0: 0, 1: 1},
        compiler_params=pltpu.CompilerParams(vmem_limit_bytes=MIB),
    )(*values, done)


def owner_kernel(owners, *refs):
    count = owners.shape[0]
    kinds = len(refs) // 4
    for i in range(kinds):
        factor, sib_factor, out, across = refs[i::kinds]
        clip = factor.shape[0]
        rows = out.shape[0] // count
        across[:, :clip] = factor[...].T
        across[:, clip:] = sib_factor[...].T
        for p in range(count):
            start = pl.multiple_of(owners[p] * rows, 16)
            out[p * rows : (p + 1) * rows, :] = across[pl.ds(start, rows), :]


def owner_blocks(factors, sib_factors, bits):
    mine = lax.axis_index("dp")
    flips = [
        [
            sum(1 << bit for i, bit in enumerate(phase_bits(bits, core)) if p >> (bits - 1 - i) & 1)
            for p in range(1 << bits)
        ]
        for core in (0, 1)
    ]
    owners = mine ^ jnp.where(mine % 2 == 0, jnp.array(flips[0]), jnp.array(flips[1]))
    clip = factors[0].shape[0]
    vmem = pl.BlockSpec(memory_space=pltpu.VMEM)
    return pl.pallas_call(
        owner_kernel,
        out_shape=[jax.ShapeDtypeStruct((f.shape[1] // 2, 2 * clip), BF) for f in factors],
        in_specs=[SMEM] + [vmem] * (2 * len(factors)),
        out_specs=[vmem] * len(factors),
        scratch_shapes=[pltpu.VMEM((f.shape[1], 2 * clip), BF) for f in factors],
        compiler_params=pltpu.CompilerParams(vmem_limit_bytes=16 * MIB),
        cost_estimate=NO_COST,
    )(owners.astype(jnp.int32), *factors, *sib_factors)


def sum_to_owner(low, high, bits, factor):
    for phase in range(bits):
        arrived = lax.ppermute(high, "dp", phase_pairs(bits, phase))
        if phase + 1 == bits:
            return (low[0].astype(F32) + arrived[0].astype(F32)) * factor
        count = low.shape[0] // 2
        high = (low[count:].astype(F32) + arrived[count:].astype(F32)).astype(BF)
        low = (low[:count].astype(F32) + arrived[:count].astype(F32)).astype(BF)


def shards(
    control_in,
    base_in,
    base_update,
    out_gain,
    cotangent,
    w_qkv,
    w_out,
    w_hint,
    window_offset,
    tile_mask,
    token_layout,
):
    segments = lax.axis_size("segment")
    devices = lax.axis_size("dp")
    mine = lax.axis_index("segment")
    rows, width = control_in.shape
    feat = base_in.shape[1]
    qkv_rows, out_rows = (w_qkv.shape[1], w_out.shape[1])
    factor = float(rows * devices) ** (-0.5)
    bits = (devices // 2).bit_length() - 1
    bias = token_bias(window_offset[0], tile_mask[0], token_layout[0])
    packed, owners, bias = gather_shards(pack_shard(w_qkv[0], w_out[0]), bits, bias)
    last = devices // 2 - 1
    hint_shard, packed[last] = lax.optimization_barrier((w_hint[0], packed[last]))
    weight_hint = lax.all_gather(hint_shard, "dp", axis=0, tiled=True)
    shapes = ((devices * qkv_rows, 3 * HD), (devices * out_rows, width))
    weights = land_shards(owners, packed[:-1], 0, [], shapes)
    weights = land_shards(owners, packed[-1:], devices - 1, weights, shapes)
    flags = [jnp.where(mine == t, 1, 0).astype(jnp.int32).reshape(1) for t in range(segments)]

    state = unwritten(
        ((rows, width), BF),
        ((rows, HEAD), F32),
        ((rows, 3 * HD), BF),
        ((HEADS, rows, rows), BF),
        ((rows, HD), BF),
        ((rows, width), BF),
    )
    half = rows // 2
    moving = [base_in[:half], base_in[half:]]
    arriving, deps = (control_in, [])

    def add_term(t, moving, state, after=()):
        terms = hint_term(flags[t], base_update[0], state[5], weight_hint, after)
        return [add_rows(m, term) for m, term in zip(moving, terms)]

    for t in range(segments):
        if t > 1:
            deps = add_term(t - 1, moving, state)
            moving = [lax.ppermute(m, "segment", [(t - 1, t)]) for m in deps]
        state, send = forward_section(flags[t], arriving, weights, bias, state, deps)
        if t + 1 < segments:
            arriving = lax.ppermute(send, "segment", [(t, t + 1)])
        if t == 1:
            sums = add_term(0, moving, state, (arriving,))
            moving = [lax.ppermute(m, "segment", [(0, 1)]) for m in sums]
    summed = add_term(segments - 1, moving, state)
    normed, inv, proj, probs, att, ctl = state

    top = unwritten(((rows, feat), F32), ((rows, feat), BF), ((rows, width), BF))
    back = unwritten(((rows, width), BF), ((rows, width), BF), ((rows, 3 * HD), BF))
    gain = out_gain[None]
    owners = devices // 2
    grad_next, deps = (None, [])
    for t in range(segments):
        s = segments - 1 - t
        below = [lax.ppermute(m, "segment", [(s, s - 1)]) for m in summed] if s else None
        held = []
        if s:
            top = top_section(flags[s], summed, cotangent, gain, weight_hint, top, deps)
        if s == 1:
            top = top_section(flags[0], below, cotangent, gain, weight_hint, top, [])
            hint = owner_products(
                product_kernel, (ctl_rows, top[1], sibling(top[1])), owners, qkv_rows, feat
            )
            held = hint[1:]
        back = backward_section(
            flags[s], grad_next, top[2], weights, (normed, inv, proj, probs), back, held
        )
        deps = [back[2]]
        if s:
            grad_next = lax.ppermute(back[0], "segment", [(s, s - 1)])
        if t == 1:
            factors, _ = lax.optimization_barrier(((normed, att, ctl), back[2]))
            norm_rows, att_rows, ctl_rows = owner_blocks(
                factors, [sibling(f) for f in factors], bits
            )
            deps = [back[2], norm_rows]
        summed = held_until(below, back[1]) if t and s > 1 else below
    _, after, gproj = back
    after_sib, gproj_sib = (sibling(after), sibling(gproj))
    first = owner_products(
        out_value_kernel,
        (att_rows, after, after_sib, norm_rows, gproj, gproj_sib),
        owners,
        2 * out_rows,
        width,
    )
    second = owner_products(
        product_kernel, (norm_rows, gproj, gproj_sib), owners, qkv_rows, 2 * HD
    )
    first = sum_to_owner(*first, bits, factor)
    second = sum_to_owner(*second, bits, factor)
    third = sum_to_owner(*hint, bits, factor)
    value = jnp.concatenate((first[out_rows:, :HD], first[out_rows:, HD:]), 0)
    return (
        top[0],
        jnp.concatenate((second, value), 1)[None],
        first[None, :out_rows],
        third[None],
    )


def solution(mesh):
    placed = (
        P("dp", None),
        P("dp", None),
        P("segment", "dp", None),
        P(),
        P("dp", None),
        P("segment", "dp", None),
        P("segment", "dp", None),
        P("segment", "dp", None),
        P("segment", None),
        P("segment", None, None),
        P("dp", None),
    )
    return jax.shard_map(
        shards,
        mesh=mesh,
        in_specs=placed,
        out_specs=(
            P("dp", None),
            P("segment", "dp", None),
            P("segment", "dp", None),
            P("segment", "dp", None),
        ),
        check_vma=False,
    )
```

time: 898 us -> 473 us (0.53)
  waiting for transfers between devices: 669 us -> 231 us
  Pallas kernels: 0 us -> 125 us
  matrix products: 51.2 us -> 1.73 us
  local copies, waits for them, and re-layouts: 61.4 us -> 28.6 us
  starting transfers between devices: 77.7 us -> 58.1 us
  other arithmetic: 22.8 us -> 4.15 us
    reduce_scatter x3 -> x0, waiting for transfers between devices: 169 us -> none  [the longest x1 70.3 us: shards(): lax.psum_scatter(local_grads[2].astype(jnp.bfloat16), 'dp', scatter_dimen...]
    all_gather x3 -> x1, waiting for transfers between devices: 136 us -> 0.02 us  [shards(): weight_hint = lax.all_gather(hint_shard, 'dp', axis=0, tiled=True)]
    pallas_call x0 -> x35, Pallas kernels: none -> 125 us  [the longest x2 75 us: land_shards(): pl.pallas_call(functools.partial(land_kernel, first, count), out_shape=[j...]
    psum x1 -> x0, waiting for transfers between devices: 89.1 us -> none  [shards(): lax.psum(term.astype(jnp.bfloat16), 'segment').astype(jnp.float32)]
    dot_general x14 -> x1, matrix products: 49.4 us -> 1.73 us  [token_bias(): pairs = jnp.dot(jnp.dot(member, permitted), member.T)]
    ppermute x8 -> x37, waiting for transfers between devices: 273 us -> 231 us  [the longest x6 68.9 us: shards(): lax.ppermute(m, 'segment', [(s, s - 1)])]
    unnamed x16 -> x110, local copies, waits for them, and re-layouts: 0.17 us -> 27 us
    while x7 -> x0, local copies, waits for them, and re-layouts: 19.7 us -> none  [the longest x3 16.1 us: shards(): local_grads = lax.fori_loop(0, segments, backward_turn, start_back)[1]]
  transfers between devices with their start and end apart: 15 -> 38, of which waited for: 15 -> 14; matrix products, arithmetic and copies ran while one was open for 2% -> 1% of each run, Pallas kernels for 0% -> 24%
where the time goes in v1:
time: 473 us; the launch traced here: 464 us
  waiting for transfers between devices  231 us (49%)
  Pallas kernels  125 us (26%)
  starting transfers between devices  58.1 us (12%)
  local copies, waits for them, and re-layouts  28.6 us (6%)
  between operations  15.5 us (3%)
    pallas_call x2, Pallas kernels, land_shards(): pl.pallas_call(functools.partial(land_kernel, first, count), out_shape=[j...  75 us
    ppermute x6, waiting for transfers between devices, shards(): lax.ppermute(m, 'segment', [(s, s - 1)])  68.9 us
    ppermute x6, waiting for transfers between devices, sum_to_owner(): arrived = lax.ppermute(high, 'dp', phase_pairs(bits, phase))  45.6 us
    pallas_call x16, Pallas kernels, call(): pl.pallas_call(kernel, out_shape=outs, in_specs=specs, out_specs=out_spec...  41.4 us
    ppermute x3, waiting for transfers between devices, gather_shards(): lax.ppermute(held[p ^ 1 << phase], 'dp', phase_pairs(bits, phase))  36.8 us
    ppermute x3, waiting for transfers between devices, shards(): grad_next = lax.ppermute(back[0], 'segment', [(s, s - 1)])  30.3 us
    ppermute x2, starting transfers between devices, shards(): moving = [lax.ppermute(m, 'segment', [(0, 1)]) for m in sums]  27.5 us
    unnamed x110, local copies, waits for them, and re-layouts  27 us
  transfers between devices with their start and end apart: 38, of which 14 were waited for; matrix products, arithmetic and copies ran while one was open for 1% of the time, Pallas kernels for 24%

profile of v1, /device:TPU:0, one launch (start us, length us, event | category | flops | bytes accessed | tf_op | source)
XLA Modules:
  0.0 463.6 jit_solution(1987448959878370553)
XLA Ops:
  7.2 1.2 copy-done.26
  9.7 3.0 collective-permute-start
  12.7 1.5 collective-permute-start.1
  14.3 1.7 fusion.bias
  16.0 22.9 %collective-permute-done.refs_1_ = bf16[256,2304]{1,0:T(8,128)(2,1)S(1)} collective-permute-done((bf16[256,2304]{1,0:T(8,128)(2,1)S(1)}, bf16[256,2304]{1,0:T(8,128)(2,1)S(1)}, u32[]{:S(2)}, u32[]{:S(2)}) %collective-permute-start) | collective-permute-done | bytes 1179680 | tf_op jit(solution)/shard_map/ppermute | solution.py:114
  38.9 1.6 collective-permute-start.3
  41.2 13.9 %collective-permute-done.3.refs_3_ = bf16[256,2304]{1,0:T(8,128)(2,1)S(1)} collective-permute-done((bf16[256,2304]{1,0:T(8,128)(2,1)S(1)}, bf16[256,2304]{1,0:T(8,128)(2,1)S(1)}, u32[]{:S(2)}, u32[]{:S(2)}) %collective-permute-start.3) | collective-permute-done | bytes 1179680 | tf_op jit(solution)/shard_map/ppermute | solution.py:114
  57.7 1.3 copy-done.21
  59.0 1.3 copy-done.23
  60.3 1.3 copy-done.25
  61.5 37.5 %shard_map.175 = (bf16[1536,2304]{1,0:T(8,128)(2,1)}, bf16[768,1536]{1,0:T(8,128)(2,1)}) custom-call(s32[8]{0:T(128)S(1)} %fusion.19.owners, bf16[256,2304]{1,0:T(8,128)(2,1)S(1)} %shard_map.174.refs_0_, bf16[256,2304]{1,0:T(8,128)(2,1)S(1)} %collective-permute-done.refs_1_, bf16[256,2304]{1,0:T(8,128)(2,1)S(1)} %collective-permute-done.1.refs_2_, ...), custom_call_target="tpu_custom_call" | custom-call | tf_op jit(solution)/shard_map/pallas_call | solution.py:160
  99.0 37.5 %shard_map.176 = (bf16[1536,2304]{1,0:T(8,128)(2,1)}, bf16[768,1536]{1,0:T(8,128)(2,1)}) custom-call(s32[8]{0:T(128)} %copy-done.36, bf16[256,2304]{1,0:T(8,128)(2,1)} %collective-permute-done.6.refs_0_, bf16[1536,2304]{1,0:T(8,128)(2,1)} %get-tuple-element.111.refs_1_, ...), custom_call_target="tpu_custom_call", output_to_operand_aliasing={{0}: (2, {}), {1}: (3, {})} | custom-call | tf_op jit(solution)/shard_map/pallas_call | solution.py:160
  136.6 10.3 %shard_map.178 = (bf16[256,1536]{1,0:T(8,128)(2,1)}, f32[256,128]{1,0:T(8,128)}, bf16[256,2304]{1,0:T(8,128)(2,1)}, bf16[6,256,256]{2,1,0:T(8,128)(2,1)}, bf16[2...) custom-call(s32[1]{0:T(128)} %bitcast.flag, ...), custom_call_target="tpu_custom_call", output_to_operand_aliasing={{0}: (5, {}), {1}: (6, {}), {2}: (7, {}), {3}: (8, {}), {4}... | custom-call | tf_op jit(solution)/shard_map/pallas_call | solution.py:194
  146.8 1.3 collective-permute-start.7
  148.2 17.9 %collective-permute-done.7.x = bf16[256,1536]{1,0:T(8,128)(2,1)S(1)} collective-permute-done((bf16[256,1536]{1,0:T(8,128)(2,1)}, bf16[256,1536]{1,0:T(8,128)(2,1)S(1)}, u32[]{:S(2)}, u32[]{:S(2)}) %collective-permute-start.7) | collective-permute-done | bytes 786464 | tf_op jit(solution)/shard_map/ppermute | solution.py:678
  169.3 6.1 %shard_map.180 = (bf16[128,2560]{1,0:T(8,128)(2,1)}, bf16[128,2560]{1,0:T(8,128)(2,1)}) custom-call(s32[1]{0:T(128)} %bitcast.flag, bf16[256,2560]{1,0:T(8,128)(2,1)} %bitcast.23, bf16[256,1536]{1,0:T(8,128)(2,1)} %get-tuple-element.128.ctl.refs_5_, bf16[1536,2560]{1,0:T(8,128)(2,1)} %all-gather.2.cloned.1.call-done.weight, bf16[256,1536]{1,0:T(8,128)(2,1)} %copy-done.37), custom_call_target="tpu_custom_call" | custom-call | tf_op jit(solution)/shard_map/pallas_call | solution.py:194
  175.5 1.1 copy-done.34
  176.8 26.1 %collective-permute-start.11 = (bf16[128,2560]{1,0:T(8,128)(2,1)S(1)}, bf16[128,2560]{1,0:T(8,128)(2,1)S(1)}, u32[]{:S(2)}, u32[]{:S(2)}) collective-permute-start(bf16[128,2560]{1,0:T(8,128)(2,1)S(1)} %shard_map.184), channel_id=1, source_target_pairs={{0,8},{1,9},{2,10},{3,11},{4,12},{5,13},{6,14},{7,15}} | collective-permute-start | bytes 1966088 | tf_op jit(solution)/shard_map/ppermute | solution.py:681
  203.1 1.3 collective-permute-start.9
  204.6 13.3 %collective-permute-done.11.one = bf16[128,2560]{1,0:T(8,128)(2,1)S(1)} collective-permute-done((bf16[128,2560]{1,0:T(8,128)(2,1)S(1)}, bf16[128,2560]{1,0:T(8,128)(2,1)S(1)}, u32[]{:S(2)}, u32[]{:S(2)}) %collective-permute-start.11) | collective-permute-done | bytes 655392 | tf_op jit(solution)/shard_map/ppermute | solution.py:681
  219.8 10.4 %collective-permute-done.9.one = bf16[128,2560]{1,0:T(8,128)(2,1)S(1)} collective-permute-done((bf16[128,2560]{1,0:T(8,128)(2,1)S(1)}, bf16[128,2560]{1,0:T(8,128)(2,1)S(1)}, u32[]{:S(2)}, u32[]{:S(2)}) %collective-permute-start.9) | collective-permute-done | bytes 655392 | tf_op jit(solution)/shard_map/ppermute | solution.py:681
  240.3 2.5 shard_map.197
  246.2 3.8 shard_map.199
  251.7 1.3 collective-permute-start.21
  253.0 1.3 collective-permute-start.22
  254.5 1.6 collective-permute-done.24.refs_4_
  256.1 1.7 shard_map.201
  258.9 59.0 %collective-permute-done.21.upper = bf16[128,2560]{1,0:T(8,128)(2,1)S(1)} collective-permute-done((bf16[128,2560]{1,0:T(8,128)(2,1)S(1)}, bf16[128,2560]{1,0:T(8,128)(2,1)S(1)}, u32[]{:S(2)}, u32[]{:S(2)}) %collective-permute-start.21) | collective-permute-done | bytes 655392 | tf_op jit(solution)/shard_map/ppermute | solution.py:692
  317.9 9.8 %collective-permute-done.22.lower = bf16[128,2560]{1,0:T(8,128)(2,1)S(1)} collective-permute-done((bf16[128,2560]{1,0:T(8,128)(2,1)S(1)}, bf16[128,2560]{1,0:T(8,128)(2,1)S(1)}, u32[]{:S(2)}, u32[]{:S(2)}) %collective-permute-start.22) | collective-permute-done | bytes 655392 | tf_op jit(solution)/shard_map/ppermute | solution.py:692
  328.7 7.2 %shard_map.203 = (f32[256,2560]{1,0:T(8,128)}, bf16[256,2560]{1,0:T(8,128)(2,1)}, bf16[256,1536]{1,0:T(8,128)(2,1)}) custom-call(s32[1]{0:T(128)} %bitcast.flag, bf16[128,2560]{1,0:T(8,128)(2,1)} %copy-done.47, bf16[128,2560]{1,0:T(8,128)(2,1)} %copy-done.48, bf16[256,2560]{1,0:T(8,128)(2,1)} %cot.7, ...), custom_call_target="tpu_custom_call", output_to_operand_aliasing={{0}: (6, {}), {1}: (7, {}), {2}: (8, {})} | custom-call | tf_op jit(solution)/shard_map/pallas_call | solution.py:194
  336.7 2.5 collective-permute-done.27.gproj_sib
  339.2 1.3 copy-done.4
  340.5 2.2 shard_map.204
  342.7 1.3 copy-done.18
  345.0 1.4 collective-permute-start.28
  346.5 2.5 collective-permute-start.35
  349.0 30.3 %collective-permute-done.28.refs_0_ = bf16[256,1536]{1,0:T(8,128)(2,1)S(1)} collective-permute-done((bf16[256,1536]{1,0:T(8,128)(2,1)}, bf16[256,1536]{1,0:T(8,128)(2,1)S(1)}, u32[]{:S(2)}, u32[]{:S(2)}) %collective-permute-start.28) | collective-permute-done | bytes 786464 | tf_op jit(solution)/shard_map/ppermute | solution.py:707
  380.2 10.1 %shard_map.206 = (bf16[256,1536]{1,0:T(8,128)(2,1)}, bf16[256,1536]{1,0:T(8,128)(2,1)}, bf16[256,2304]{1,0:T(8,128)(2,1)}) custom-call(s32[1]{0:T(128)} %bitcast.flag, bf16[1536,2304]{1,0:T(8,128)(2,1)} %get-tuple-element.113.w_qkv, bf16[768,1536]{1,0:T(8,128)(2,1)} %get-tuple-element.114.w_out, ...), custom_call_target="tpu_custom_call", output_to_operand_aliasing={{1}: (10, {}), {2}: (11, {})} | custom-call | tf_op jit(solution)/shard_map/pallas_call | solution.py:194
  390.9 3.7 collective-permute-done.32.after_sib
  394.5 1.3 copy-done
  396.9 1.4 shard_map.208
  398.3 2.5 collective-permute-start.33
  402.2 1.4 shard_map.207
  403.7 21.9 %collective-permute-done.33 = bf16[2,192,1536]{2,1,0:T(8,128)(2,1)S(1)} collective-permute-done((bf16[2,192,1536]{2,1,0:T(8,128)(2,1)S(1)}, bf16[2,192,1536]{2,1,0:T(8,128)(2,1)S(1)}, u32[]{:S(2)}, u32[]{:S(2)}) %collective-permute-start.33) | collective-permute-done | bytes 1179680 | tf_op jit(solution)/shard_map/ppermute | solution.py:617
  426.9 1.7 add_multiply_fusion
  428.5 16.0 %collective-permute-done.30 = bf16[2,192,1536]{2,1,0:T(8,128)(2,1)S(1)} collective-permute-done((bf16[2,192,1536]{2,1,0:T(8,128)(2,1)S(1)}, bf16[2,192,1536]{2,1,0:T(8,128)(2,1)S(1)}, u32[]{:S(2)}, u32[]{:S(2)}) %collective-permute-start.30) | collective-permute-done | bytes 1179680 | tf_op jit(solution)/shard_map/ppermute | solution.py:617
  447.0 7.7 %collective-permute-done.31 = bf16[1,192,1536]{2,1,0:T(8,128)(2,1)S(1)} collective-permute-done((bf16[1,192,1536]{2,1,0:T(8,128)(2,1)S(1)}, bf16[1,192,1536]{2,1,0:T(8,128)(2,1)S(1)}, u32[]{:S(2)}, u32[]{:S(2)}) %collective-permute-start.31) | collective-permute-done | bytes 589856 | tf_op jit(solution)/shard_map/ppermute | solution.py:617
  455.0 1.3 maximum_bitcast_fusion
  (190 shorter events, 36.8 us)
Async XLA Ops:
  7.2 161.3 %all-gather.2.cloned.1.call-start = ((), (), s32[]{:S(2)}) async-start(), calls=%async_computation | async-start | bytes 8847360 | tf_op jit(solution)/shard_map/all_gather | solution.py:650
  9.6 48.1 %copy-start.51 = (s32[8]{0:T(128)S(1)}, s32[8]{0:T(128)}, u32[]{:S(2)}) copy-start(s32[8]{0:T(128)} %constant.62.clone) | copy-start | bytes 100
  9.6 48.1 %copy-start.52 = (s32[8]{0:T(128)S(1)}, s32[8]{0:T(128)}, u32[]{:S(2)}) copy-start(s32[8]{0:T(128)} %constant.63.clone) | copy-start | bytes 100
  9.7 29.3 %collective-permute-start = (bf16[256,2304]{1,0:T(8,128)(2,1)S(1)}, bf16[256,2304]{1,0:T(8,128)(2,1)S(1)}, u32[]{:S(2)}, u32[]{:S(2)}) collective-permute-start(bf16[256,2304]{1,0:T(8,128)(2,1)S(1)} %shard_map.174.refs_0_), channel_id=1, source_target_pairs={{0,2},{1,5},{2,0},{3,7},{4,6},{5,1},{6,4},{7,3},{8,10},{9,13},{10,... | collective-permute-start | bytes 3538952 | tf_op jit(solution)/shard_map/ppermute | solution.py:114
  12.7 26.3 %collective-permute-start.1 = (bf16[256,2304]{1,0:T(8,128)(2,1)S(1)}, bf16[256,2304]{1,0:T(8,128)(2,1)S(1)}, u32[]{:S(2)}, u32[]{:S(2)}) collective-permute-start(bf16[256,2304]{1,0:T(8,128)(2,1)S(1)} %shard_map.174.refs_0_), channel_id=1, source_target_pairs={{0,4},{1,3},{2,6},{3,1},{4,0},{5,7},{6,2},{7,5},{8,12},{9,11},{10,... | collective-permute-start | bytes 3538952 | tf_op jit(solution)/shard_map/ppermute | solution.py:114
  14.2 24.7 %collective-permute-start.2 = (bf16[256,2304]{1,0:T(8,128)(2,1)S(1)}, bf16[256,2304]{1,0:T(8,128)(2,1)}, u32[]{:S(2)}, u32[]{:S(2)}) collective-permute-start(bf16[256,2304]{1,0:T(8,128)(2,1)S(1)} %shard_map.174.refs_0_), channel_id=1, source_target_pairs={{0,1},{1,0},{2,3},{3,2},{4,5},{5,4},{6,7},{7,6},{8,9},{9,8},{10,11... | collective-permute-start | bytes 3538952 | tf_op jit(solution)/shard_map/ppermute | solution.py:103
  38.9 16.2 %collective-permute-start.3 = (bf16[256,2304]{1,0:T(8,128)(2,1)S(1)}, bf16[256,2304]{1,0:T(8,128)(2,1)S(1)}, u32[]{:S(2)}, u32[]{:S(2)}) collective-permute-start(bf16[256,2304]{1,0:T(8,128)(2,1)S(1)} %collective-permute-done.refs_1_), channel_id=1, source_target_pairs={{0,4},{1,3},{2,6},{3,1},{4,0},{5,7},{6,2},{7,5},{8,12},{9,11},{10,... | collective-permute-start | bytes 3538952 | tf_op jit(solution)/shard_map/ppermute | solution.py:114
  40.5 14.6 %collective-permute-start.4 = (bf16[256,2304]{1,0:T(8,128)(2,1)S(1)}, bf16[256,2304]{1,0:T(8,128)(2,1)S(1)}, u32[]{:S(2)}, u32[]{:S(2)}) collective-permute-start(bf16[256,2304]{1,0:T(8,128)(2,1)S(1)} %collective-permute-done.refs_1_), channel_id=1, source_target_pairs={{0,1},{1,0},{2,3},{3,2},{4,5},{5,4},{6,7},{7,6},{8,9},{9,8},{10,11... | collective-permute-start | bytes 3538952 | tf_op jit(solution)/shard_map/ppermute | solution.py:103
  41.2 15.0 %collective-permute-start.5 = (bf16[256,2304]{1,0:T(8,128)(2,1)S(1)}, bf16[256,2304]{1,0:T(8,128)(2,1)S(1)}, u32[]{:S(2)}, u32[]{:S(2)}) collective-permute-start(bf16[256,2304]{1,0:T(8,128)(2,1)S(1)} %collective-permute-done.1.refs_2_), channel_id=1, source_target_pairs={{0,1},{1,0},{2,3},{3,2},{4,5},{5,4},{6,7},{7,6},{8,9},{9,8},{10,11... | collective-permute-start | bytes 3538952 | tf_op jit(solution)/shard_map/ppermute | solution.py:103
  57.6 41.5 %collective-permute-start.6 = (bf16[256,2304]{1,0:T(8,128)(2,1)}, bf16[256,2304]{1,0:T(8,128)(2,1)}, u32[]{:S(2)}, u32[]{:S(2)}) collective-permute-start(bf16[256,2304]{1,0:T(8,128)(2,1)} %copy-done.20), channel_id=1, source_target_pairs={{0,1},{1,0},{2,3},{3,2},{4,5},{5,4},{6,7},{7,6},{8,9},{9,8},{10,11... | collective-permute-start | bytes 3538952 | tf_op jit(solution)/shard_map/ppermute | solution.py:103
  61.5 37.5 %copy-start.36 = (s32[8]{0:T(128)}, s32[8]{0:T(128)S(1)}, u32[]{:S(2)}) copy-start(s32[8]{0:T(128)S(1)} %fusion.19.owners) | copy-start | bytes 100
  146.8 19.3 %collective-permute-start.7 = (bf16[256,1536]{1,0:T(8,128)(2,1)}, bf16[256,1536]{1,0:T(8,128)(2,1)S(1)}, u32[]{:S(2)}, u32[]{:S(2)}) collective-permute-start(bf16[256,1536]{1,0:T(8,128)(2,1)} %get-tuple-element.121), channel_id=1, source_target_pairs={{0,8},{1,9},{2,10},{3,11},{4,12},{5,13},{6,14},{7,15}} | collective-permute-start | bytes 2359304 | tf_op jit(solution)/shard_map/ppermute | solution.py:678
  167.1 1.3 collective-permute-start.8
  175.4 27.5 %copy-start.30 = (bf16[128,2560]{1,0:T(8,128)(2,1)S(1)}, bf16[128,2560]{1,0:T(8,128)(2,1)}, u32[]{:S(2)}) copy-start(bf16[128,2560]{1,0:T(8,128)(2,1)} %get-tuple-element.131.two) | copy-start | bytes 1966084
  176.8 41.1 %collective-permute-start.11 = (bf16[128,2560]{1,0:T(8,128)(2,1)S(1)}, bf16[128,2560]{1,0:T(8,128)(2,1)S(1)}, u32[]{:S(2)}, u32[]{:S(2)}) collective-permute-start(bf16[128,2560]{1,0:T(8,128)(2,1)S(1)} %shard_map.184), channel_id=1, source_target_pairs={{0,8},{1,9},{2,10},{3,11},{4,12},{5,13},{6,14},{7,15}} | collective-permute-start | bytes 1966088 | tf_op jit(solution)/shard_map/ppermute | solution.py:681
  203.1 27.1 %collective-permute-start.9 = (bf16[128,2560]{1,0:T(8,128)(2,1)S(1)}, bf16[128,2560]{1,0:T(8,128)(2,1)S(1)}, u32[]{:S(2)}, u32[]{:S(2)}) collective-permute-start(bf16[128,2560]{1,0:T(8,128)(2,1)S(1)} %shard_map.181), channel_id=1, source_target_pairs={{0,8},{1,9},{2,10},{3,11},{4,12},{5,13},{6,14},{7,15}} | collective-permute-start | bytes 1966088 | tf_op jit(solution)/shard_map/ppermute | solution.py:681
  204.6 25.6 %copy-start.27 = (bf16[128,2560]{1,0:T(8,128)(2,1)S(1)}, bf16[128,2560]{1,0:T(8,128)(2,1)}, u32[]{:S(2)}) copy-start(bf16[128,2560]{1,0:T(8,128)(2,1)} %get-tuple-element.132.two) | copy-start | bytes 1966084
  219.1 12.0 %copy-start.15 = (bf16[128,2560]{1,0:T(8,128)(2,1)}, bf16[128,2560]{1,0:T(8,128)(2,1)S(1)}, u32[]{:S(2)}) copy-start(bf16[128,2560]{1,0:T(8,128)(2,1)S(1)} %shard_map.185.refs_7_) | copy-start | bytes 1966084
  219.1 13.1 %collective-permute-start.14 = (bf16[128,2560]{1,0:T(8,128)(2,1)S(1)}, bf16[128,2560]{1,0:T(8,128)(2,1)S(1)}, u32[]{:S(2)}, u32[]{:S(2)}) collective-permute-start(bf16[128,2560]{1,0:T(8,128)(2,1)S(1)} %shard_map.185.refs_7_), channel_id=1, source_target_pairs={{8,16},{9,17},{10,18},{11,19},{12,20},{13,21},{14,22},{15,23}} | collective-permute-start | bytes 1966088 | tf_op jit(solution)/shard_map/ppermute | solution.py:675
  230.3 3.9 collective-permute-start.10
  231.3 3.8 collective-permute-start.13
  233.5 3.0 collective-permute-start.17
  234.4 4.3 collective-permute-start.12
  237.8 5.8 %collective-permute-start.18 = (bf16[128,2560]{1,0:T(8,128)(2,1)S(1)}, bf16[128,2560]{1,0:T(8,128)(2,1)S(1)}, u32[]{:S(2)}, u32[]{:S(2)}) collective-permute-start(bf16[128,2560]{1,0:T(8,128)(2,1)S(1)} %shard_map.193.lower), channel_id=1, source_target_pairs={{24,16},{25,17},{26,18},{27,19},{28,20},{29,21},{30,22},{31,23}} | collective-permute-start | bytes 1966088 | tf_op jit(solution)/shard_map/ppermute | solution.py:692
  238.9 5.5 %collective-permute-start.15 = (bf16[128,2560]{1,0:T(8,128)(2,1)S(1)}, bf16[128,2560]{1,0:T(8,128)(2,1)S(1)}, u32[]{:S(2)}, u32[]{:S(2)}) collective-permute-start(bf16[128,2560]{1,0:T(8,128)(2,1)S(1)} %shard_map.192.upper), channel_id=1, source_target_pairs={{24,16},{25,17},{26,18},{27,19},{28,20},{29,21},{30,22},{31,23}} | collective-permute-start | bytes 1966088 | tf_op jit(solution)/shard_map/ppermute | solution.py:692
  242.9 2.4 collective-permute-start.20
  243.6 7.0 %collective-permute-start.19 = (bf16[128,2560]{1,0:T(8,128)(2,1)S(1)}, bf16[128,2560]{1,0:T(8,128)(2,1)S(1)}, u32[]{:S(2)}, u32[]{:S(2)}) collective-permute-start(bf16[128,2560]{1,0:T(8,128)(2,1)S(1)} %collective-permute-done.18.lower), channel_id=1, source_target_pairs={{16,8},{17,9},{18,10},{19,11},{20,12},{21,13},{22,14},{23,15}} | collective-permute-start | bytes 1966088 | tf_op jit(solution)/shard_map/ppermute | solution.py:692
  244.3 6.3 %collective-permute-start.16 = (bf16[128,2560]{1,0:T(8,128)(2,1)S(1)}, bf16[128,2560]{1,0:T(8,128)(2,1)S(1)}, u32[]{:S(2)}, u32[]{:S(2)}) collective-permute-start(bf16[128,2560]{1,0:T(8,128)(2,1)S(1)} %collective-permute-done.15.upper), channel_id=1, source_target_pairs={{16,8},{17,9},{18,10},{19,11},{20,12},{21,13},{22,14},{23,15}} | collective-permute-start | bytes 1966088 | tf_op jit(solution)/shard_map/ppermute | solution.py:692
  246.2 8.2 %copy-start.7 = (bf16[256,768]{1,0:T(8,128)(2,1)S(1)}, bf16[256,768]{1,0:T(8,128)(2,1)}, u32[]{:S(2)}) copy-start(bf16[256,768]{1,0:T(8,128)(2,1)} %get-tuple-element.177.refs_1_) | copy-start | bytes 1179652
  250.0 6.1 %collective-permute-start.23 = (bf16[256,1536]{1,0:T(8,128)(2,1)S(1)}, bf16[256,1536]{1,0:T(8,128)(2,1)S(1)}, u32[]{:S(2)}, u32[]{:S(2)}) collective-permute-start(bf16[256,1536]{1,0:T(8,128)(2,1)S(1)} %copy-done.2), channel_id=1, source_target_pairs={{0,1},{1,0},{2,3},{3,2},{4,5},{5,4},{6,7},{7,6},{8,9},{9,8},{10,11... | collective-permute-start | bytes 2359304 | tf_op jit(solution)/shard_map/ppermute | solution.py:103
  250.1 6.0 %collective-permute-start.25 = (bf16[256,1536]{1,0:T(8,128)(2,1)S(1)}, bf16[256,1536]{1,0:T(8,128)(2,1)S(1)}, u32[]{:S(2)}, u32[]{:S(2)}) collective-permute-start(bf16[256,1536]{1,0:T(8,128)(2,1)S(1)} %copy-done.3), channel_id=1, source_target_pairs={{0,1},{1,0},{2,3},{3,2},{4,5},{5,4},{6,7},{7,6},{8,9},{9,8},{10,11... | collective-permute-start | bytes 2359304 | tf_op jit(solution)/shard_map/ppermute | solution.py:103
  251.7 66.2 %collective-permute-start.21 = (bf16[128,2560]{1,0:T(8,128)(2,1)S(1)}, bf16[128,2560]{1,0:T(8,128)(2,1)S(1)}, u32[]{:S(2)}, u32[]{:S(2)}) collective-permute-start(bf16[128,2560]{1,0:T(8,128)(2,1)S(1)} %get-tuple-element.170.upper), channel_id=1, source_target_pairs={{8,0},{9,1},{10,2},{11,3},{12,4},{13,5},{14,6},{15,7}} | collective-permute-start | bytes 1966088 | tf_op jit(solution)/shard_map/ppermute | solution.py:692
  253.0 74.7 %collective-permute-start.22 = (bf16[128,2560]{1,0:T(8,128)(2,1)S(1)}, bf16[128,2560]{1,0:T(8,128)(2,1)S(1)}, u32[]{:S(2)}, u32[]{:S(2)}) collective-permute-start(bf16[128,2560]{1,0:T(8,128)(2,1)S(1)} %get-tuple-element.171.lower), channel_id=1, source_target_pairs={{8,0},{9,1},{10,2},{11,3},{12,4},{13,5},{14,6},{15,7}} | collective-permute-start | bytes 1966088 | tf_op jit(solution)/shard_map/ppermute | solution.py:692
  254.3 1.8 collective-permute-start.24
  317.9 9.8 %copy-start.47 = (bf16[128,2560]{1,0:T(8,128)(2,1)}, bf16[128,2560]{1,0:T(8,128)(2,1)S(1)}, u32[]{:S(2)}) copy-start(bf16[128,2560]{1,0:T(8,128)(2,1)S(1)} %collective-permute-done.21.upper) | copy-start | bytes 1966084
  328.7 7.3 %copy-start.43 = (bf16[256,1536]{1,0:T(8,128)(2,1)S(1)}, bf16[256,1536]{1,0:T(8,128)(2,1)}, u32[]{:S(2)}) copy-start(bf16[256,1536]{1,0:T(8,128)(2,1)} %get-tuple-element.184.refs_6_) | copy-start | bytes 2359300
  335.9 3.3 collective-permute-start.27
  336.0 8.0 %collective-permute-start.26 = (bf16[256,1536]{1,0:T(8,128)(2,1)S(1)}, bf16[256,1536]{1,0:T(8,128)(2,1)S(1)}, u32[]{:S(2)}, u32[]{:S(2)}) collective-permute-start(bf16[256,1536]{1,0:T(8,128)(2,1)S(1)} %copy-done.43), channel_id=1, source_target_pairs={{16,8},{17,9},{18,10},{19,11},{20,12},{21,13},{22,14},{23,15}} | collective-permute-start | bytes 2359304 | tf_op jit(solution)/shard_map/ppermute | solution.py:707
  345.0 34.3 %collective-permute-start.28 = (bf16[256,1536]{1,0:T(8,128)(2,1)}, bf16[256,1536]{1,0:T(8,128)(2,1)S(1)}, u32[]{:S(2)}, u32[]{:S(2)}) collective-permute-start(bf16[256,1536]{1,0:T(8,128)(2,1)} %get-tuple-element.189.refs_6_), channel_id=1, source_target_pairs={{8,0},{9,1},{10,2},{11,3},{12,4},{13,5},{14,6},{15,7}} | collective-permute-start | bytes 2359304 | tf_op jit(solution)/shard_map/ppermute | solution.py:707
  346.5 54.4 %collective-permute-start.35 = (bf16[2,192,2560]{2,1,0:T(8,128)(2,1)S(1)}, bf16[2,192,2560]{2,1,0:T(8,128)(2,1)S(1)}, u32[]{:S(2)}, u32[]{:S(2)}) collective-permute-start(bf16[2,192,2560]{2,1,0:T(8,128)(2,1)S(1)} %copy-done.19), channel_id=1, source_target_pairs={{0,2},{1,5},{2,0},{3,7},{4,6},{5,1},{6,4},{7,3},{8,10},{9,13},{10,... | collective-permute-start | bytes 5898248 | tf_op jit(solution)/shard_map/ppermute | solution.py:617
  380.2 14.4 %copy-start.9 = (bf16[768,512]{1,0:T(8,128)(2,1)S(1)}, bf16[768,512]{1,0:T(8,128)(2,1)}, u32[]{:S(2)}) copy-start(bf16[768,512]{1,0:T(8,128)(2,1)} %copy-done.8) | copy-start | bytes 2359300
  390.3 4.3 collective-permute-start.29
  390.4 4.2 collective-permute-start.32
  398.3 27.3 %collective-permute-start.33 = (bf16[2,192,1536]{2,1,0:T(8,128)(2,1)S(1)}, bf16[2,192,1536]{2,1,0:T(8,128)(2,1)S(1)}, u32[]{:S(2)}, u32[]{:S(2)}) collective-permute-start(bf16[2,192,1536]{2,1,0:T(8,128)(2,1)S(1)} %get-tuple-element.198), channel_id=1, source_target_pairs={{0,2},{1,5},{2,0},{3,7},{4,6},{5,1},{6,4},{7,3},{8,10},{9,13},{10,... | collective-permute-start | bytes 3538952 | tf_op jit(solution)/shard_map/ppermute | solution.py:617
  401.1 25.7 %collective-permute-start.36 = (bf16[1,192,2560]{2,1,0:T(8,128)(2,1)S(1)}, bf16[1,192,2560]{2,1,0:T(8,128)(2,1)S(1)}, u32[]{:S(2)}, u32[]{:S(2)}) collective-permute-start(bf16[1,192,2560]{2,1,0:T(8,128)(2,1)S(1)} %add_convert_fusion), channel_id=1, source_target_pairs={{0,4},{1,3},{2,6},{3,1},{4,0},{5,7},{6,2},{7,5},{8,12},{9,11},{10,... | collective-permute-start | bytes 2949128 | tf_op jit(solution)/shard_map/ppermute | solution.py:617
  403.6 41.0 %collective-permute-start.30 = (bf16[2,192,1536]{2,1,0:T(8,128)(2,1)S(1)}, bf16[2,192,1536]{2,1,0:T(8,128)(2,1)S(1)}, u32[]{:S(2)}, u32[]{:S(2)}) collective-permute-start(bf16[2,192,1536]{2,1,0:T(8,128)(2,1)S(1)} %get-tuple-element.194), channel_id=1, source_target_pairs={{0,2},{1,5},{2,0},{3,7},{4,6},{5,1},{6,4},{7,3},{8,10},{9,13},{10,... | collective-permute-start | bytes 3538952 | tf_op jit(solution)/shard_map/ppermute | solution.py:617
  425.7 20.1 %collective-permute-start.34 = (bf16[1,192,1536]{2,1,0:T(8,128)(2,1)S(1)}, bf16[1,192,1536]{2,1,0:T(8,128)(2,1)S(1)}, u32[]{:S(2)}, u32[]{:S(2)}) collective-permute-start(bf16[1,192,1536]{2,1,0:T(8,128)(2,1)S(1)} %add_convert_fusion.2), channel_id=1, source_target_pairs={{0,4},{1,3},{2,6},{3,1},{4,0},{5,7},{6,2},{7,5},{8,12},{9,11},{10,... | collective-permute-start | bytes 1769480 | tf_op jit(solution)/shard_map/ppermute | solution.py:617
  444.8 9.9 %collective-permute-start.31 = (bf16[1,192,1536]{2,1,0:T(8,128)(2,1)S(1)}, bf16[1,192,1536]{2,1,0:T(8,128)(2,1)S(1)}, u32[]{:S(2)}, u32[]{:S(2)}) collective-permute-start(bf16[1,192,1536]{2,1,0:T(8,128)(2,1)S(1)} %add_convert_fusion.4), channel_id=1, source_target_pairs={{0,4},{1,3},{2,6},{3,1},{4,0},{5,7},{6,2},{7,5},{8,12},{9,11},{10,... | collective-permute-start | bytes 1769480 | tf_op jit(solution)/shard_map/ppermute | solution.py:617
  (45 other events, 81.1 us)
Sparse Core Ops, SparseCore 0:
  57.7 53.6 all-gather.1
